TPU v7x, 32 devices: a whole 2x2x4 slice. The times are simulated.
32 devices in a mesh: dp: 8 (over z, x), seq: 4 (over y, core).
Axes of the slice: x: 2, y: 2, z: 4, core: 2. Of those that a mesh axis runs over, the one named last changes fastest.
Arguments:
- tokens: bfloat16 [8, 1024, 768], P('dp', 'seq'), may hold values from -6 to 6
- norm_gain: float32 [768], P('dp'), may hold values from 0.5 to 1.5
- in_weight: bfloat16 [768, 3352], P('dp'), may hold values from -0.21875 to 0.21875
- conv_weight: float32 [4, 1792], P(None, 'dp'), may hold values from -3 to 3
- conv_bias: float32 [1792], P('dp'), may hold values from -0.5 to 0.5
- dt_bias: float32 [24], replicated, may hold values from -4.5 to -3
- a_log: float32 [24], replicated, as said below
- skip: float32 [24], replicated, may hold values from 0.5 to 1.5
- gate_norm: float32 [1536], P('dp'), may hold values from 0.5 to 1.5
- out_weight: bfloat16 [1536, 768], P('dp'), may hold values from -0.15625 to 0.15625
- cotangent: bfloat16 [8, 1024, 768], P('dp', 'seq'), may hold values from -6 to 6
Outputs:
- mixed: bfloat16 [8, 1024, 768], P('dp', 'seq')
- grad_tokens: bfloat16 [8, 1024, 768], P('dp', 'seq')
- grad_norm_gain: float32 [768], P('dp')
- grad_in_weight: float32 [768, 3352], P('dp')
- grad_conv_weight: float32 [4, 1792], P(None, 'dp')
- grad_conv_bias: float32 [1792], P('dp')
- grad_dt_bias: float32 [24], replicated
- grad_a_log: float32 [24], replicated
- grad_skip: float32 [24], replicated
- grad_gate_norm: float32 [1536], P('dp')
- grad_out_weight: float32 [1536, 768], P('dp')
Inputs may be any that keep to these rules, and one draw needn't show every extreme that they name: exp(a_log) lies between 4 / 1024 and 0.6.
All inputs are finite; a program needn't handle non-finite values.
Results may differ from a plain program's by a relative error of at most 0.018.
Values may be sent and summed in bfloat16 or wider, within the bound.
A program may use at most 128 MiB of HBM per device.

v0:
```python
import jax
import jax.numpy as jnp
from jax import lax
from jax.sharding import PartitionSpec as P

HEADS = 24
HEAD = 64
STATE = 128
KCONV = 4


EPS = 1e-05


def passed_along(block, axis, distance):
    devices = range(lax.axis_size(axis))
    route = [(i - distance, i) for i in devices if i - distance in devices]
    return lax.ppermute(block, axis, route)


def silu_slope(value):
    sig = jax.nn.sigmoid(value)
    return sig * (1.0 + value * (1.0 - sig))


def gather_weights(in_weight, out_weight):
    return (
        lax.all_gather(in_weight, "dp", axis=0, tiled=True),
        lax.all_gather(out_weight, "dp", axis=0, tiled=True),
    )


def carry_states(decay, local, reverse):
    moved = jnp.zeros_like(local)
    for step in range(lax.axis_size("seq") - 1):
        if reverse:
            moved = passed_along(decay[:, :, None, None] * moved + local, "seq", -1)
        else:
            moved = passed_along(decay[:, :, None, None] * moved + local, "seq", 1)
    return moved


def body(
    tokens,
    norm_gain,
    in_weight,
    conv_weight,
    conv_bias,
    dt_bias,
    a_log,
    skip,
    gate_norm,
    out_weight,
    cotangent,
):
    seqs, piece, width = tokens.shape
    inner = HEADS * HEAD
    chans = inner + 2 * STATE
    edge_rows = KCONV - 1
    f32 = jnp.float32
    b16 = jnp.bfloat16
    norm_full, conv_full, cbias_full, gnorm_full = (
        lax.all_gather(norm_gain, "dp", axis=0, tiled=True),
        lax.all_gather(conv_weight, "dp", axis=1, tiled=True),
        lax.all_gather(conv_bias, "dp", axis=0, tiled=True),
        lax.all_gather(gate_norm, "dp", axis=0, tiled=True),
    )
    w_in, w_out = gather_weights(in_weight, out_weight)
    x_in = tokens.astype(f32)
    rinv = lax.rsqrt(jnp.mean(x_in * x_in, -1, keepdims=True) + EPS)
    unit = x_in * rinv
    h16 = (unit * norm_full).astype(b16)
    proj = jnp.einsum("sqd,de->sqe", h16, w_in, preferred_element_type=f32)
    zval = proj[..., :inner]
    xbc16 = proj[..., inner : inner + chans].astype(b16)
    dt_raw = proj[..., inner + chans :]
    edge = passed_along(xbc16[:, piece - edge_rows :, :], "seq", 1)
    padded16 = jnp.concatenate([edge, xbc16], 1)
    pre = cbias_full + conv_full[0] * padded16[:, 0:piece]
    for k in range(1, KCONV):
        pre = pre + conv_full[k] * padded16[:, k : k + piece]
    xconv = jax.nn.silu(pre)
    xs16 = xconv[..., :inner].astype(b16).reshape(seqs, piece, HEADS, HEAD)
    bm16 = xconv[..., inner : inner + STATE].astype(b16)
    cm16 = xconv[..., inner + STATE :].astype(b16)
    shifted = dt_raw + dt_bias
    dth = jnp.swapaxes(jax.nn.softplus(shifted), 1, 2)
    rate = -jnp.exp(a_log)
    cumh = jnp.cumsum(dth * rate[None, :, None], axis=2)
    lower = jnp.arange(piece)[:, None] >= jnp.arange(piece)[None, :]
    seg = jnp.where(lower, cumh[:, :, :, None] - cumh[:, :, None, :], -1e30)
    lmat = jnp.exp(seg)
    gram = jnp.einsum("stn,sun->stu", cm16, bm16, preferred_element_type=f32)
    w16 = (gram[:, None] * lmat * dth[:, :, None, :]).astype(b16)
    y_diag = jnp.einsum("shtu,suhp->sthp", w16, xs16, preferred_element_type=f32)
    endc = cumh[:, :, -1]
    ewt = jnp.exp(endc[:, :, None] - cumh)
    factor = ewt * dth
    bw16 = (bm16[:, None] * factor[..., None]).astype(b16)
    s_loc = jnp.einsum("shun,suhp->shpn", bw16, xs16, preferred_element_type=f32)
    decay = jnp.exp(endc)
    s_in = carry_states(decay, s_loc, False)
    s_in16 = s_in.astype(b16)
    ecum = jnp.exp(cumh)
    ce16 = (cm16[:, None] * ecum[..., None]).astype(b16)
    y_off = jnp.einsum("shtn,shpn->sthp", ce16, s_in16, preferred_element_type=f32)
    xsf = xs16.astype(f32)
    yval = (y_diag + y_off + skip[:, None] * xsf).reshape(seqs, piece, inner)
    gate_act = jax.nn.silu(zval)
    gated = yval * gate_act
    grinv = lax.rsqrt(jnp.mean(gated * gated, -1, keepdims=True) + EPS)
    gunit = gated * grinv
    n16 = (gunit * gnorm_full).astype(b16)
    branch = jnp.einsum("sqi,id->sqd", n16, w_out, preferred_element_type=f32)
    mixed = (x_in + branch).astype(b16)
    g_wout = jnp.einsum("sqi,sqd->id", n16, cotangent, preferred_element_type=f32)
    dnorm = jnp.einsum("sqd,id->sqi", cotangent, w_out, preferred_element_type=f32)
    g_gnorm = jnp.sum(dnorm * gunit, (0, 1))
    dscaled = dnorm * gnorm_full
    dgated = grinv * (dscaled - gunit * jnp.mean(dscaled * gunit, -1, keepdims=True))
    dy16 = (dgated * gate_act).astype(b16).reshape(seqs, piece, HEADS, HEAD)
    dz = dgated * yval * silu_slope(zval)
    dyf = dy16.astype(f32)
    g_skip = jnp.sum(dyf * xsf, (0, 1, 3))
    dxs = skip[:, None] * dyf
    dce = jnp.einsum("sthp,shpn->shtn", dy16, s_in16, preferred_element_type=f32)
    ds_loc_in = jnp.einsum("shtn,sthp->shpn", ce16, dy16, preferred_element_type=f32)
    dcm = jnp.sum(dce * ecum[..., None], 1)
    dcum = jnp.sum(dce * cm16[:, None] * ecum[..., None], -1)
    ds_out = carry_states(decay, ds_loc_in, True)
    dsl16 = ds_out.astype(b16)
    dend = jnp.sum(ds_out * s_in, (2, 3)) * decay
    dbw = jnp.einsum("shpn,suhp->shun", dsl16, xs16, preferred_element_type=f32)
    dxs = dxs + jnp.einsum("shun,shpn->suhp", bw16, dsl16, preferred_element_type=f32)
    dbm = jnp.sum(dbw * factor[..., None], 1)
    dfactor = jnp.sum(dbw * bm16[:, None], -1)
    ddt = dfactor * ewt
    dlog = dfactor * factor
    dend = dend + jnp.sum(dlog, -1)
    dcum = dcum - dlog
    dwmat = jnp.einsum("sthp,suhp->shtu", dy16, xs16, preferred_element_type=f32)
    dxs = dxs + jnp.einsum("shtu,sthp->suhp", w16, dy16, preferred_element_type=f32)
    dlmat = dwmat * gram[:, None] * dth[:, :, None, :]
    dg16 = jnp.sum(dwmat * lmat * dth[:, :, None, :], 1).astype(b16)
    ddt = ddt + jnp.sum(dwmat * gram[:, None] * lmat, 2)
    dseg = dlmat * lmat
    dcum = dcum + jnp.sum(dseg, 3) - jnp.sum(dseg, 2)
    dcm = dcm + jnp.einsum("stu,sun->stn", dg16, bm16, preferred_element_type=f32)
    dbm = dbm + jnp.einsum("stu,stn->sun", dg16, cm16, preferred_element_type=f32)
    dcum = dcum + jnp.pad(dend[..., None], ((0, 0), (0, 0), (piece - 1, 0)))
    dda = jnp.flip(jnp.cumsum(jnp.flip(dcum, 2), 2), 2)
    ddt = ddt + dda * rate[None, :, None]
    g_alog = jnp.sum(dda * dth, (0, 2)) * rate
    draw = jnp.swapaxes(ddt, 1, 2) * jax.nn.sigmoid(shifted)
    g_dtb = jnp.sum(draw, (0, 1))
    dxconv = jnp.concatenate([dxs.reshape(seqs, piece, inner), dbm, dcm], -1)
    dpre = dxconv * silu_slope(pre)
    g_cbias = jnp.sum(dpre, (0, 1))
    g_conv = jnp.stack([jnp.sum(dpre * padded16[:, k : k + piece], (0, 1)) for k in range(KCONV)])
    dpadded = jnp.pad(conv_full[0] * dpre, ((0, 0), (0, edge_rows), (0, 0)))
    for k in range(1, KCONV):
        dpadded = dpadded + jnp.pad(conv_full[k] * dpre, ((0, 0), (k, edge_rows - k), (0, 0)))
    returned = passed_along(dpadded[:, :edge_rows], "seq", -1)
    dxbc = dpadded[:, edge_rows:] + jnp.pad(returned, ((0, 0), (piece - edge_rows, 0), (0, 0)))
    dproj16 = jnp.concatenate([dz, dxbc, draw], -1).astype(b16)
    g_win = jnp.einsum("sqd,sqe->de", h16, dproj16, preferred_element_type=f32)
    dhid = jnp.einsum("sqe,de->sqd", dproj16, w_in, preferred_element_type=f32)
    g_norm = jnp.sum(dhid * unit, (0, 1))
    dunit = dhid * norm_full
    dx_in = cotangent.astype(f32) + rinv * (
        dunit - unit * jnp.mean(dunit * unit, -1, keepdims=True)
    )
    grad_tokens = dx_in.astype(b16)
    owned = (
        lax.psum_scatter(g_norm.astype(jnp.bfloat16), "dp", scatter_dimension=0, tiled=True).astype(
            jnp.float32
        ),
        lax.psum_scatter(g_win.astype(jnp.bfloat16), "dp", scatter_dimension=0, tiled=True).astype(
            jnp.float32
        ),
        lax.psum_scatter(g_conv.astype(jnp.bfloat16), "dp", scatter_dimension=1, tiled=True).astype(
            jnp.float32
        ),
        lax.psum_scatter(
            g_cbias.astype(jnp.bfloat16), "dp", scatter_dimension=0, tiled=True
        ).astype(jnp.float32),
        lax.psum_scatter(
            g_gnorm.astype(jnp.bfloat16), "dp", scatter_dimension=0, tiled=True
        ).astype(jnp.float32),
        lax.psum_scatter(g_wout.astype(jnp.bfloat16), "dp", scatter_dimension=0, tiled=True).astype(
            jnp.float32
        ),
    )
    owned = (
        lax.psum(owned[0].astype(jnp.bfloat16), "seq").astype(jnp.float32),
        lax.psum(owned[1].astype(jnp.bfloat16), "seq").astype(jnp.float32),
        lax.psum(owned[2].astype(jnp.bfloat16), "seq").astype(jnp.float32),
        lax.psum(owned[3].astype(jnp.bfloat16), "seq").astype(jnp.float32),
        lax.psum(owned[4].astype(jnp.bfloat16), "seq").astype(jnp.float32),
        lax.psum(owned[5].astype(jnp.bfloat16), "seq").astype(jnp.float32),
    )
    head_sums = lax.psum((g_dtb, g_alog, g_skip), ("dp", "seq"))
    return (
        mixed,
        grad_tokens,
        owned[0],
        owned[1],
        owned[2],
        owned[3],
        head_sums[0],
        head_sums[1],
        head_sums[2],
        owned[4],
        owned[5],
    )


def solution(mesh):
    placed = (
        P("dp", "seq", None),
        P("dp"),
        P("dp", None),
        P(None, "dp"),
        P("dp"),
        P(),
        P(),
        P(),
        P("dp"),
        P("dp", None),
        P("dp", "seq", None),
    )
    return jax.shard_map(
        body,
        mesh=mesh,
        in_specs=placed,
        out_specs=(
            P("dp", "seq", None),
            P("dp", "seq", None),
            P("dp"),
            P("dp", None),
            P(None, "dp"),
            P("dp"),
            P(),
            P(),
            P(),
            P("dp"),
            P("dp", None),
        ),
        check_vma=False,
    )
```

profile of v0, /device:TPU:0, one launch (start us, length us, event | category | flops | bytes accessed | tf_op | source)
XLA Modules:
  0.0 522.0 jit_solution(1525503781313008762)
XLA Ops:
  13.7 32.9 %all-gather = f32[8,224,4]{1,2,0:T(4,128)S(1)} all-gather(f32[1,224,4]{1,2,0:T(4,128)} %bitcast.239), channel_id=1, replica_groups=mesh['dp'=8,'seq'=4] {'dp'}, dimensions={0}, use_global_device_ids=true | all-gather | bytes 32256 | tf_op jit(solution)/shard_map/all_gather | solution.py:64
  51.2 38.5 %all-reduce.13 = (f32[768]{0:T(1024)}, f32[1792]{0:T(1024)}, f32[1536]{0:T(1024)S(1)}) all-reduce(f32[768]{0:T(1024)S(1)} %dynamic-update-slice.1, f32[1792]{0:T(1024)S(1)} %dynamic-update-slice, f32[1536]{0:T(1024)S(1)} %dynamic-update-slice.2), channel_id=1, replica_groups=mesh['dp'=8,'seq'=4] {'dp'}, use_global_device_ids=true, to_apply=%add.7 | all-reduce | flops 4096 | bytes 32768
  89.6 11.5 %all-gather.4.cloned.1.call-done = bf16[768,3352]{1,0:T(8,128)(2,1)} async-done(((bf16[96,3352]{1,0:T(8,128)(2,1)}), bf16[768,3352]{1,0:T(8,128)(2,1)}) %all-gather.4.cloned.1.call-update) | async-done | bytes 5148688 | tf_op jit(solution)/shard_map/all_gather | solution.py:28
  101.2 5.6 %fusion.92 = (bf16[1,256,3352]{2,1,0:T(8,128)(2,1)}, f32[1,256,3352]{2,1,0:T(8,128)S(1)}) fusion(bf16[768,3352]{1,0:T(8,128)(2,1)} %all-gather.4.cloned.1.call-done, bf16[1,256,768]{2,1,0:T(8,128)(2,1)} %param.11, f32[768]{0:T(1024)} %get-tuple-element.38, f32[256]{0:T(256)} %add_rsqrt_fusion.1), kind=kOutput, calls=%fused_computation.186 | convolution fusion | flops 1319704576 | bytes 10694656 | tf_op jit(solution)/shard_map/sqd,de->sqe/dot_general | solution.py:73
  127.1 3.8 multiply_convert_fusion.9
  139.3 3.6 collective-permute-start.1
  145.8 9.8 %collective-permute-start.2 = (f32[1,24,64,128]{3,2,1,0:T(8,128)}, f32[1,24,64,128]{3,2,1,0:T(8,128)}, u32[]{:S(2)}, u32[]{:S(2)}) collective-permute-start(f32[1,24,64,128]{3,2,1,0:T(8,128)} %bitcast_add_fusion.6), channel_id=1, source_target_pairs={{0,1},{1,2},{2,3},{4,5},{5,6},{6,7},{8,9},{9,10},{10,11},{12,13},{... | collective-permute-start | bytes 2359304 | tf_op jit(solution)/shard_map/ppermute | solution.py:18
  160.9 9.3 %collective-permute-start.3 = (f32[1,24,64,128]{3,2,1,0:T(8,128)S(1)}, f32[1,24,64,128]{3,2,1,0:T(8,128)S(1)}, u32[]{:S(2)}, u32[]{:S(2)}) collective-permute-start(f32[1,24,64,128]{3,2,1,0:T(8,128)S(1)} %bitcast_add_fusion.5), channel_id=1, source_target_pairs={{0,1},{1,2},{2,3},{4,5},{5,6},{6,7},{8,9},{9,10},{10,11},{12,13},{... | collective-permute-start | bytes 2359304 | tf_op jit(solution)/shard_map/ppermute | solution.py:18
  186.7 4.4 multiply_reduce_fusion.6
  196.7 6.5 %collective-permute-done.4 = f32[1,24,64,128]{3,2,1,0:T(8,128)S(1)} collective-permute-done((f32[1,24,64,128]{3,2,1,0:T(8,128)S(1)}, f32[1,24,64,128]{3,2,1,0:T(8,128)S(1)}, u32[]{:S(2)}, u32[]{:S(2)}) %collective-permute-start.4) | collective-permute-done | bytes 786464 | tf_op jit(solution)/shard_map/ppermute | solution.py:18
  205.8 5.5 %fusion.1 = (f32[24,256]{1,0:T(8,128)}, f32[24,256]{1,0:T(8,128)}, f32[24,256]{1,0:T(8,128)}, bf16[256,256]{1,0:T(8,128)(2,1)}) fusion(f32[24,256]{1,0:T(8,128)S(1)} %copy-done.53, f32[24,256]{1,0:T(8,128)S(1)} %copy-done.56, f32[256,256]{1,0:T(8,128)S(1)} %copy-done.34, pred[256,256]{1,0:T(8,128)(4,1)S(1)} %copy-done.44, ...), kind=kOutput, calls=%fused_computation.8 | convolution fusion | flops 220116992 | bytes 2154496 | tf_op jit(solution)/shard_map/sthp,suhp->shtu/dot_general | solution.py:141
  232.2 6.6 %collective-permute-done.6 = f32[1,24,64,128]{3,2,1,0:T(8,128)S(1)} collective-permute-done((f32[1,24,64,128]{3,2,1,0:T(8,128)S(1)}, f32[1,24,64,128]{3,2,1,0:T(8,128)S(1)}, u32[]{:S(2)}, u32[]{:S(2)}) %collective-permute-start.6) | collective-permute-done | bytes 786464 | tf_op jit(solution)/shard_map/ppermute | solution.py:18
  260.9 3.3 bitcast_add_fusion
  268.5 4.8 fusion.86
  277.7 9.0 %collective-permute-done.7 = f32[1,3,1792]{2,0,1:T(1,128)S(1)} collective-permute-done((f32[1,3,1792]{2,0,1:T(1,128)S(1)}, f32[1,3,1792]{2,0,1:T(1,128)S(1)}, u32[]{:S(2)}, u32[]{:S(2)}) %collective-permute-start.7) | collective-permute-done | bytes 21536 | tf_op jit(solution)/shard_map/ppermute | solution.py:18
  287.8 4.1 convolution_convert_fusion
  294.2 3.3 fusion.30
  299.8 43.5 %all-reduce.12 = (f32[24]{0:T(128)}, f32[24]{0:T(128)}, f32[24]{0:T(128)}) all-reduce(f32[24]{0:T(128)S(1)} %copy-done.78, f32[24]{0:T(128)S(1)} %fusion.82, f32[24]{0:T(128)S(1)} %reduce_sum.268), channel_id=1, replica_groups=mesh['dp'=8,'seq'=4] {'dp','seq'}, use_global_device_ids=true, to_apply=%region_33.34 | all-reduce | flops 72 | bytes 576 | tf_op jit(solution)/shard_map/psum | solution.py:202
  343.3 4.6 fusion.44
  347.9 37.0 %all-reduce.14 = (bf16[768]{0:T(1024)(128)(2,1)S(1)}, bf16[1792]{0:T(1024)(128)(2,1)S(1)}, bf16[1536]{0:T(1024)(128)(2,1)S(1)}) all-reduce(bf16[768]{0:T(1024)(128)(2,1)S(1)} %get-tuple-element.29, bf16[1792]{0:T(1024)(128)(2,1)S(1)} %copy-done.60, bf16[1536]{0:T(1024)(128)(2,1)S(1)} %copy-done.59), channel_id=2, replica_groups=mesh['dp'=8,'seq'=4] {'dp'}, use_global_device_ids=true, to_apply=%region_19.20.clone | all-reduce | flops 4096 | bytes 16384
  385.1 24.4 %reduce-scatter.6.cloned.1.call-done = bf16[96,3352]{1,0:T(8,128)(2,1)} async-done(((bf16[768,3352]{1,0:T(8,128)(2,1)}), bf16[96,3352]{1,0:T(8,128)(2,1)}) %reduce-scatter.6.cloned.1.call-update) | async-done | bytes 643600 | tf_op jit(solution)/shard_map/reduce_scatter | solution.py:178
  410.6 64.7 %reduce-scatter.10.cloned.1.call-done = bf16[224,4]{1,0:T(8,128)(2,1)} async-done(((bf16[1792,4]{1,0:T(8,128)(2,1)}), bf16[224,4]{1,0:T(8,128)(2,1)}) %reduce-scatter.10.cloned.1.call-update) | async-done | bytes 1808
  476.2 5.7 %all-reduce.15 = (bf16[96]{0:T(256)(128)(2,1)S(1)}, bf16[4,224]{1,0:T(4,128)(2,1)S(1)}, bf16[224]{0:T(256)(128)(2,1)S(1)}, bf16[192]{0:T(256)(128)(2,1)S(1)}) all-reduce(bf16[96]{0:T(256)(128)(2,1)S(1)} %dynamic-slice.4, bf16[4,224]{1,0:T(4,128)(2,1)S(1)} %copy.190, ...), channel_id=1, replica_groups=mesh['dp'=8,'seq'=4] {'seq'}, use_global_device_ids=true, to_apply=%region_20.21 | all-reduce | flops 1408 | bytes 5632 | tf_op jit(solution)/shard_map/psum | solution.py:195
  484.1 28.0 %all-reduce.19.cloned.1.call-done = (bf16[96,3352]{1,0:T(8,128)(2,1)}, bf16[192,768]{1,0:T(8,128)(2,1)}) async-done(((bf16[96,3352]{1,0:T(8,128)(2,1)}, bf16[192,768]{1,0:T(8,128)(2,1)}), (bf16[96,3352]{1,0:T(8,128)(2,1)}, bf16[192,768]{1,0:T(8,128)(2,1)})) %all-reduce.19.cloned.1.call-update) | async-done | bytes 938512 | tf_op jit(solution)/shard_map/psum | solution.py:196
  (299 shorter events, 132.6 us)
Async XLA Ops:
  7.2 94.0 %all-gather.4.cloned.1.call-start = ((), (), s32[]{:S(2)}) async-start(), calls=%async_computation.3 | async-start | bytes 5971968 | tf_op jit(solution)/shard_map/all_gather | solution.py:28
  7.9 175.5 %all-gather.6.cloned.1.call-start = ((), (), s32[]{:S(2)}) async-start(), calls=%async_computation.4 | async-start | bytes 2654208 | tf_op jit(solution)/shard_map/all_gather | solution.py:29
  8.7 376.4 %reduce-scatter.8.cloned.1.call-start = ((), (), s32[]{:S(2)}) async-start(), calls=%async_computation.6 | async-start | bytes 2654208 | tf_op jit(solution)/shard_map/reduce_scatter | solution.py:190
  106.8 50.1 %copy-start = (f32[1,256,3352]{2,1,0:T(8,128)}, f32[1,256,3352]{2,1,0:T(8,128)S(1)}, u32[]{:S(2)}) copy-start(f32[1,256,3352]{2,1,0:T(8,128)S(1)} %get-tuple-element.73) | copy-start | bytes 10297348
  115.6 11.5 %collective-permute-start = (bf16[1,3,1792]{2,1,0:T(4,128)(2,1)}, bf16[1,3,1792]{2,1,0:T(4,128)(2,1)}, u32[]{:S(2)}, u32[]{:S(2)}) collective-permute-start(bf16[1,3,1792]{2,1,0:T(4,128)(2,1)} %slice.97), channel_id=1, source_target_pairs={{0,1},{1,2},{2,3},{4,5},{5,6},{6,7},{8,9},{9,10},{10,11},{12,13},{... | collective-permute-start | bytes 32264 | tf_op jit(solution)/shard_map/ppermute | solution.py:18
  139.1 17.1 %copy-start.31 = (f32[1,24,2,128]{3,1,2,0:T(8,128)S(1)}, f32[1,24,2,128]{3,1,2,0:T(8,128)}, u32[]{:S(2)}) copy-start(f32[1,24,2,128]{3,1,2,0:T(8,128)} %reduce-window.14) | copy-start | bytes 73732
  139.1 17.7 %copy-start.66 = (f32[24]{0:T(128)S(1)}, f32[24]{0:T(128)}, u32[]{:S(2)}) copy-start(f32[24]{0:T(128)} %param.16) | copy-start | bytes 292
  139.3 5.4 %collective-permute-start.1 = (f32[1,24,64,128]{3,2,1,0:T(8,128)S(1)}, f32[1,24,64,128]{3,2,1,0:T(8,128)S(1)}, u32[]{:S(2)}, u32[]{:S(2)}) collective-permute-start(f32[1,24,64,128]{3,2,1,0:T(8,128)S(1)} %add_bitcast_fusion.1), channel_id=1, source_target_pairs={{0,1},{1,2},{2,3},{4,5},{5,6},{6,7},{8,9},{9,10},{10,11},{12,13},{... | collective-permute-start | bytes 2359304 | tf_op jit(solution)/shard_map/ppermute | solution.py:18
  145.8 13.6 %collective-permute-start.2 = (f32[1,24,64,128]{3,2,1,0:T(8,128)}, f32[1,24,64,128]{3,2,1,0:T(8,128)}, u32[]{:S(2)}, u32[]{:S(2)}) collective-permute-start(f32[1,24,64,128]{3,2,1,0:T(8,128)} %bitcast_add_fusion.6), channel_id=1, source_target_pairs={{0,1},{1,2},{2,3},{4,5},{5,6},{6,7},{8,9},{9,10},{10,11},{12,13},{... | collective-permute-start | bytes 2359304 | tf_op jit(solution)/shard_map/ppermute | solution.py:18
  157.6 12.6 %copy-start.42 = (f32[1,24,2,128]{3,2,1,0:T(2,128)S(1)}, f32[1,24,2,128]{3,2,1,0:T(2,128)}, u32[]{:S(2)}) copy-start(f32[1,24,2,128]{3,2,1,0:T(2,128)} %copy.151) | copy-start | bytes 73732
  158.6 15.4 %copy-start.52 = (f32[24,256]{1,0:T(8,128)}, f32[24,256]{1,0:T(8,128)S(1)}, u32[]{:S(2)}) copy-start(f32[24,256]{1,0:T(8,128)S(1)} %copy.153) | copy-start | bytes 73732
  160.9 11.9 %copy-start.25 = (f32[256,128]{1,0:T(8,128)S(1)}, f32[256,128]{1,0:T(8,128)}, u32[]{:S(2)}) copy-start(f32[256,128]{1,0:T(8,128)} %get-tuple-element.65) | copy-start | bytes 393220
  160.9 16.3 %collective-permute-start.3 = (f32[1,24,64,128]{3,2,1,0:T(8,128)S(1)}, f32[1,24,64,128]{3,2,1,0:T(8,128)S(1)}, u32[]{:S(2)}, u32[]{:S(2)}) collective-permute-start(f32[1,24,64,128]{3,2,1,0:T(8,128)S(1)} %bitcast_add_fusion.5), channel_id=1, source_target_pairs={{0,1},{1,2},{2,3},{4,5},{5,6},{6,7},{8,9},{9,10},{10,11},{12,13},{... | collective-permute-start | bytes 2359304 | tf_op jit(solution)/shard_map/ppermute | solution.py:18
  195.3 8.0 %collective-permute-start.4 = (f32[1,24,64,128]{3,2,1,0:T(8,128)S(1)}, f32[1,24,64,128]{3,2,1,0:T(8,128)S(1)}, u32[]{:S(2)}, u32[]{:S(2)}) collective-permute-start(f32[1,24,64,128]{3,2,1,0:T(8,128)S(1)} %add_bitcast_fusion), channel_id=1, source_target_pairs={{1,0},{2,1},{3,2},{5,4},{6,5},{7,6},{9,8},{10,9},{11,10},{13,12},{... | collective-permute-start | bytes 2359304 | tf_op jit(solution)/shard_map/ppermute | solution.py:18
  204.3 18.4 %collective-permute-start.5 = (f32[1,24,64,128]{3,2,1,0:T(8,128)}, f32[1,24,64,128]{3,2,1,0:T(8,128)}, u32[]{:S(2)}, u32[]{:S(2)}) collective-permute-start(f32[1,24,64,128]{3,2,1,0:T(8,128)} %bitcast_add_fusion.4), channel_id=1, source_target_pairs={{1,0},{2,1},{3,2},{5,4},{6,5},{7,6},{9,8},{10,9},{11,10},{13,12},{... | collective-permute-start | bytes 2359304 | tf_op jit(solution)/shard_map/ppermute | solution.py:18
  222.6 186.9 %reduce-scatter.6.cloned.1.call-start = ((), (), s32[]{:S(2)}) async-start(), calls=%async_computation.5 | async-start | bytes 5971968 | tf_op jit(solution)/shard_map/reduce_scatter | solution.py:178
  224.1 14.7 %collective-permute-start.6 = (f32[1,24,64,128]{3,2,1,0:T(8,128)S(1)}, f32[1,24,64,128]{3,2,1,0:T(8,128)S(1)}, u32[]{:S(2)}, u32[]{:S(2)}) collective-permute-start(f32[1,24,64,128]{3,2,1,0:T(8,128)S(1)} %bitcast_add_fusion.3), channel_id=1, source_target_pairs={{1,0},{2,1},{3,2},{5,4},{6,5},{7,6},{9,8},{10,9},{11,10},{13,12},{... | collective-permute-start | bytes 2359304 | tf_op jit(solution)/shard_map/ppermute | solution.py:18
  241.0 19.9 %copy-start.7 = (f32[1,256,1536]{1,2,0:T(8,128)S(1)}, f32[1,256,1536]{1,2,0:T(8,128)}, u32[]{:S(2)}) copy-start(f32[1,256,1536]{1,2,0:T(8,128)} %copy.163) | copy-start | bytes 4718596
  274.0 12.7 %collective-permute-start.7 = (f32[1,3,1792]{2,0,1:T(1,128)S(1)}, f32[1,3,1792]{2,0,1:T(1,128)S(1)}, u32[]{:S(2)}, u32[]{:S(2)}) collective-permute-start(f32[1,3,1792]{2,0,1:T(1,128)S(1)} %copy.172), channel_id=1, source_target_pairs={{1,0},{2,1},{3,2},{5,4},{6,5},{7,6},{9,8},{10,9},{11,10},{13,12},{... | collective-permute-start | bytes 64520 | tf_op jit(solution)/shard_map/ppermute | solution.py:18
  276.0 11.8 %copy-start.3 = (bf16[1,256,768]{2,1,0:T(8,128)(2,1)S(1)}, bf16[1,256,768]{2,1,0:T(8,128)(2,1)}, u32[]{:S(2)}) copy-start(bf16[1,256,768]{2,1,0:T(8,128)(2,1)} %param.11) | copy-start | bytes 1179652
  276.0 11.8 %copy-start.17 = (bf16[256,1536]{1,0:T(8,128)(2,1)S(1)}, bf16[256,1536]{1,0:T(8,128)(2,1)}, u32[]{:S(2)}) copy-start(bf16[256,1536]{1,0:T(8,128)(2,1)} %get-tuple-element.59) | copy-start | bytes 2359300
  291.9 183.3 %reduce-scatter.10.cloned.1.call-start = ((), (), s32[]{:S(2)}) async-start(), calls=%async_computation.7 | async-start | bytes 516096
  294.2 49.1 %copy-start.47 = (bf16[1,256,24]{2,1,0:T(8,128)(2,1)S(1)}, bf16[1,256,24]{2,1,0:T(8,128)(2,1)}, u32[]{:S(2)}) copy-start(bf16[1,256,24]{2,1,0:T(8,128)(2,1)} %copy-done.46) | copy-start | bytes 36868
  299.7 212.3 %all-reduce.19.cloned.1.call-start = ((), (), s32[]{:S(2)}) async-start(), calls=%async_computation.8 | async-start | bytes 1916928 | tf_op jit(solution)/shard_map/psum | solution.py:196
  (70 other events, 349.5 us)
Sparse Core Ops, SparseCore 0:
  10.2 90.9 all-gather.3
  103.4 50.2 all-gather.5
  222.7 78.4 reduce-scatter.7
  304.7 104.7 reduce-scatter.5
  413.6 61.6 reduce-scatter.9
  477.6 34.4 all-reduce.18
where the time goes:
time: 525 us; the launch traced here: 522 us
  blocking collectives  158 us (30%)
  waiting for transfers between devices  154 us (29%)
  other arithmetic  57.2 us (11%)
  local copies, waits for them, and re-layouts  51.9 us (10%)
  matrix products  51.8 us (10%)
  starting transfers between devices  30.6 us (6%)
  between operations  19.1 us (4%)
    unnamed x2, blocking collectives  75.5 us
    unnamed x7, waiting for transfers between devices  66.1 us
    psum x1, blocking collectives, body(): head_sums = lax.psum((g_dtb, g_alog, g_skip), ('dp', 'seq'))  43.5 us
    all_gather x1, blocking collectives, body(): lax.all_gather(conv_weight, 'dp', axis=1, tiled=True)  32.9 us
    ppermute x8, starting transfers between devices, passed_along(): return lax.ppermute(block, axis, route)  30.3 us
    psum x1, waiting for transfers between devices, body(): lax.psum(owned[1].astype(jnp.bfloat16), 'seq').astype(jnp.float32)  28 us
    reduce_scatter x1, waiting for transfers between devices, body(): lax.psum_scatter(g_win.astype(jnp.bfloat16), 'dp', scatter_dimension=0, t...  24.4 us
    ppermute x8, waiting for transfers between devices, passed_along(): return lax.ppermute(block, axis, route)  24 us
  transfers between devices with their start and end apart: 14, of which 8 were waited for; matrix products, arithmetic and copies ran while one was open for 27% of the time, Pallas kernels for 0%

commit v1 on v0

v1 whole, which is shorter than its diff:
```python
import functools

import jax
import jax.numpy as jnp
from jax import lax
from jax.experimental import pallas as pl
from jax.experimental.pallas import tpu as pltpu
from jax.sharding import PartitionSpec as P

HEADS = 24
HEAD = 64
STATE = 128
KCONV = 4
EPS = 1e-05
MESH = pl.DeviceIdType.MESH
F32 = jnp.float32
B16 = jnp.bfloat16


def ring_place(device, n):
    odd = device % 2
    return (1 - odd) * (device // 2) + odd * (n - 1 - device // 2)


def ring_device(place, n):
    place = (place + n) % n
    late = (2 * place) // n
    return (1 - late) * (2 * place) + late * (2 * (n - 1 - place) + 1)


def remote(src, dst, send, recv, target):
    return pltpu.make_async_remote_copy(
        src_ref=src, dst_ref=dst, send_sem=send, recv_sem=recv, device_id=target, device_id_type=MESH
    )


def greet(targets):
    barrier = pltpu.get_barrier_semaphore()
    for target in targets:
        pl.semaphore_signal(barrier, inc=1, device_id=target, device_id_type=MESH)
    pl.semaphore_wait(barrier, len(targets))


def gather_kernel(
    n, win, wout, small, gin, gout, gsmall, ring_send, ring_recv, core_send, core_recv
):
    d = lax.axis_index("dp")
    s = lax.axis_index("seq")
    c = s % 2
    p = ring_place(d, n)
    ahead = (ring_device(p + 1, n), s)
    behind = (ring_device(p - 1, n), s)
    other = (d, s + 1 - 2 * c)
    greet([ahead, behind, other])
    up = n // 2
    down = n - 1 - up
    pending = []

    def hop(index, origin, target, first):
        sources = (
            (win.at[c], wout.at[c], small)
            if first
            else (gin.at[c, origin], gout.at[c, origin], gsmall.at[origin])
        )
        dests = (gin.at[c, origin], gout.at[c, origin], gsmall.at[origin])
        copies = [
            remote(src, dst, ring_send.at[j, index], ring_recv.at[j, index], target)
            for j, (src, dst) in enumerate(zip(sources, dests))
        ]
        for copy in copies:
            copy.start()
        return copies

    def share(index, origin):
        for j, ref in enumerate((gin, gout)):
            copy = remote(
                ref.at[c, origin],
                ref.at[c, origin],
                core_send.at[j, index],
                core_recv.at[j, index],
                other,
            )
            copy.start()
            pending.append(copy)

    cw = hop(0, d, ahead, True)
    ccw = hop(up, d, behind, True)
    gin[0, d] = win[0]
    gin[1, d] = win[1]
    gout[0, d] = wout[0]
    gout[1, d] = wout[1]
    gsmall[d] = small[...]
    sent = list(cw) + list(ccw)
    for k in range(up):
        for copy in cw:
            copy.wait_recv()
        origin = ring_device(p - 1 - k, n)
        if k + 1 < up:
            cw = hop(k + 1, origin, ahead, False)
            sent += cw
        share(k, origin)
        if k < down:
            for copy in ccw:
                copy.wait_recv()
            origin = ring_device(p + 1 + k, n)
            if k + 1 < down:
                ccw = hop(up + k + 1, origin, behind, False)
                sent += ccw
            share(up + k, origin)
    for copy in sent:
        copy.wait_send()
    for copy in pending:
        copy.wait_send()
        copy.wait_recv()


def gather_all(win, wout, small, n):
    _, rows, cols = win.shape
    _, orows, ocols = wout.shape
    srows = small.shape[0]
    vmem = pl.BlockSpec(memory_space=pltpu.VMEM)
    return pl.pallas_call(
        functools.partial(gather_kernel, n),
        out_shape=(
            jax.ShapeDtypeStruct((2, n, rows, cols), B16),
            jax.ShapeDtypeStruct((2, n, orows, ocols), B16),
            jax.ShapeDtypeStruct((n, srows, 128), F32),
        ),
        in_specs=[vmem] * 3,
        out_specs=(vmem,) * 3,
        scratch_shapes=[
            pltpu.SemaphoreType.DMA((3, n - 1)),
            pltpu.SemaphoreType.DMA((3, n - 1)),
            pltpu.SemaphoreType.DMA((2, n - 1)),
            pltpu.SemaphoreType.DMA((2, n - 1)),
        ],
        compiler_params=pltpu.CompilerParams(
            collective_id=0, has_side_effects=True, vmem_limit_bytes=40 * 2**20
        ),
        name="gather_weights",
    )(win, wout, small)


def reduce_kernel(
    n,
    ny,
    pin,
    pout,
    psmall,
    phead,
    oin,
    oout,
    osmall,
    ohead,
    cin,
    cout,
    csmall,
    chead,
    sin,
    sout,
    ssmall,
    rin,
    rout,
    rsmall,
    hall,
    yin,
    yout,
    ysmall,
    yhead,
    fin,
    fout,
    core_send,
    core_recv,
    small_send,
    small_recv,
    ring_send,
    ring_recv,
    y_send,
    y_recv,
    end_send,
    end_recv,
):
    d = lax.axis_index("dp")
    s = lax.axis_index("seq")
    c = s % 2
    y = s // 2
    p = ring_place(d, n)
    ahead = (ring_device(p + 1, n), s)
    behind = (ring_device(p - 1, n), s)
    other = (d, s + 1 - 2 * c)
    peers = [(d, ((y + j) % ny) * 2 + c) for j in range(1, ny)]
    greet([ahead, behind, other] + peers)
    up = n // 2
    down = n - 1 - up
    sent = []

    small_copies = [
        remote(psmall, csmall, small_send.at[0], small_recv.at[0], other),
        remote(phead, chead, small_send.at[1], small_recv.at[1], other),
    ]
    for copy in small_copies:
        copy.start()
    order = []
    for k in range(up):
        order.append(up - k)
        if k < down:
            order.append(k - down)
    order.append(0)
    swaps = {}
    for j, offset in enumerate(order):
        t = ring_device(p + offset, n)
        swaps[offset] = [
            remote(pin.at[1 - c, t], cin.at[t], core_send.at[0, j], core_recv.at[0, j], other),
            remote(pout.at[1 - c, t], cout.at[t], core_send.at[1, j], core_recv.at[1, j], other),
        ]
        for copy in swaps[offset]:
            copy.start()
    for copy in small_copies:
        copy.wait()
    hall[d] = phead[...] + chead[...]

    def partial(offset):
        for copy in swaps[offset]:
            copy.wait_recv()
        t = ring_device(p + offset, n)
        return (
            t,
            pin[c, t].astype(F32) + cin[t].astype(F32),
            pout[c, t].astype(F32) + cout[t].astype(F32),
            psmall[t] + csmall[t],
        )

    def hop(slot, offset, before, origin, target):
        t, a, b, e = partial(offset)
        if before is not None:
            a = a + rin[before].astype(F32)
            b = b + rout[before].astype(F32)
            e = e + rsmall[before]
        sin[t] = a.astype(B16)
        sout[t] = b.astype(B16)
        ssmall[t] = e
        pairs = (
            (sin.at[t], rin.at[slot]),
            (sout.at[t], rout.at[slot]),
            (ssmall.at[t], rsmall.at[slot]),
            (hall.at[origin], hall.at[origin]),
        )
        copies = [
            remote(src, dst, ring_send.at[j, slot], ring_recv.at[j, slot], target)
            for j, (src, dst) in enumerate(pairs)
        ]
        for copy in copies:
            copy.start()
        sent.extend(copies)
        return copies

    cw = None
    ccw = None
    for k in range(up):
        if cw is not None:
            for copy in cw:
                copy.wait_recv()
        cw = hop(k, up - k, k - 1 if k else None, ring_device(p - k, n), ahead)
        if k < down:
            if ccw is not None:
                for copy in ccw:
                    copy.wait_recv()
            slot = up + k
            ccw = hop(slot, k - down, slot - 1 if k else None, ring_device(p + k, n), behind)
    _, a, b, e = partial(0)
    for copy in ccw:
        copy.wait_recv()
    last = up + down - 1
    a = a + rin[last].astype(F32)
    b = b + rout[last].astype(F32)
    e = e + rsmall[last]
    for copy in cw:
        copy.wait_recv()
    a = a + rin[up - 1].astype(F32)
    b = b + rout[up - 1].astype(F32)
    e = e + rsmall[up - 1]
    head = hall[0]
    for j in range(1, n):
        head = head + hall[j]
    yin[y] = a.astype(B16)
    yout[y] = b.astype(B16)
    ysmall[y] = e
    yhead[y] = head
    across = []
    for i, peer in enumerate(peers):
        for j, ref in enumerate((yin, yout, ysmall, yhead)):
            copy = remote(ref.at[y], ref.at[y], y_send.at[j, i], y_recv.at[j, i], peer)
            copy.start()
            across.append(copy)
    for copy in across:
        copy.wait_recv()
    a = yin[0].astype(F32)
    b = yout[0].astype(F32)
    e = ysmall[0]
    head = yhead[0]
    for j in range(1, ny):
        a = a + yin[j].astype(F32)
        b = b + yout[j].astype(F32)
        e = e + ysmall[j]
        head = head + yhead[j]
    fin[c] = a.astype(B16)
    fout[c] = b.astype(B16)
    ends = [
        remote(fin.at[c], fin.at[c], end_send.at[0], end_recv.at[0], other),
        remote(fout.at[c], fout.at[c], end_send.at[1], end_recv.at[1], other),
    ]
    for copy in ends:
        copy.start()
    osmall[...] = e
    ohead[...] = head
    for offset in order:
        for copy in swaps[offset]:
            copy.wait_send()
    for copy in sent:
        copy.wait_send()
    for copy in across:
        copy.wait_send()
    for copy in ends:
        copy.wait()
    oin[...] = fin[...].astype(F32)
    oout[...] = fout[...].astype(F32)


def reduce_all(pin, pout, psmall, phead, n, ny):
    _, _, rows, cols = pin.shape
    _, _, orows, ocols = pout.shape
    srows = psmall.shape[1]
    vmem = pl.BlockSpec(memory_space=pltpu.VMEM)
    many = max(ny - 1, 1)
    return pl.pallas_call(
        functools.partial(reduce_kernel, n, ny),
        out_shape=(
            jax.ShapeDtypeStruct((2, rows, cols), F32),
            jax.ShapeDtypeStruct((2, orows, ocols), F32),
            jax.ShapeDtypeStruct((srows, 128), F32),
            jax.ShapeDtypeStruct((8, 128), F32),
        ),
        in_specs=[vmem] * 4,
        out_specs=(vmem,) * 4,
        scratch_shapes=[
            pltpu.VMEM((n, rows, cols), B16),
            pltpu.VMEM((n, orows, ocols), B16),
            pltpu.VMEM((n, srows, 128), F32),
            pltpu.VMEM((8, 128), F32),
            pltpu.VMEM((n, rows, cols), B16),
            pltpu.VMEM((n, orows, ocols), B16),
            pltpu.VMEM((n, srows, 128), F32),
            pltpu.VMEM((n - 1, rows, cols), B16),
            pltpu.VMEM((n - 1, orows, ocols), B16),
            pltpu.VMEM((n - 1, srows, 128), F32),
            pltpu.VMEM((n, 8, 128), F32),
            pltpu.VMEM((ny, rows, cols), B16),
            pltpu.VMEM((ny, orows, ocols), B16),
            pltpu.VMEM((ny, srows, 128), F32),
            pltpu.VMEM((ny, 8, 128), F32),
            pltpu.VMEM((2, rows, cols), B16),
            pltpu.VMEM((2, orows, ocols), B16),
            pltpu.SemaphoreType.DMA((2, n)),
            pltpu.SemaphoreType.DMA((2, n)),
            pltpu.SemaphoreType.DMA((2,)),
            pltpu.SemaphoreType.DMA((2,)),
            pltpu.SemaphoreType.DMA((4, n - 1)),
            pltpu.SemaphoreType.DMA((4, n - 1)),
            pltpu.SemaphoreType.DMA((4, many)),
            pltpu.SemaphoreType.DMA((4, many)),
            pltpu.SemaphoreType.DMA((2,)),
            pltpu.SemaphoreType.DMA((2,)),
        ],
        compiler_params=pltpu.CompilerParams(
            collective_id=1, has_side_effects=True, vmem_limit_bytes=48 * 2**20
        ),
        name="reduce_gradients",
    )(pin, pout, psmall, phead)


def passed_along(block, axis, distance):
    devices = range(lax.axis_size(axis))
    route = [(i - distance, i) for i in devices if i - distance in devices]
    return lax.ppermute(block, axis, route)


def silu_slope(value):
    sig = jax.nn.sigmoid(value)
    return sig * (1.0 + value * (1.0 - sig))


def carry_states(decay, local, reverse):
    moved = jnp.zeros_like(local)
    for step in range(lax.axis_size("seq") - 1):
        total = (decay[:, None, None] * moved.astype(F32) + local).astype(B16)
        moved = passed_along(total, "seq", -1 if reverse else 1)
    return moved.astype(F32)


def dot(spec, left, right):
    return jnp.einsum(spec, left, right, preferred_element_type=F32)


def body(
    tokens,
    norm_gain,
    in_weight,
    conv_weight,
    conv_bias,
    dt_bias,
    a_log,
    skip,
    gate_norm,
    out_weight,
    cotangent,
):
    seqs, piece, width = tokens.shape
    n = lax.axis_size("dp")
    ny = lax.axis_size("seq") // 2
    inner = HEADS * HEAD
    chans = inner + 2 * STATE
    rows = in_weight.shape[0]
    orows = out_weight.shape[0]
    edge_rows = KCONV - 1
    spare = chans - inner - HEADS
    half = width // 2
    tokens = tokens[0]
    cotangent = cotangent[0]

    win = jnp.stack(
        [
            in_weight[:, inner : inner + chans],
            jnp.concatenate(
                [
                    in_weight[:, :inner],
                    in_weight[:, inner + chans :],
                    jnp.zeros((rows, spare), B16),
                ],
                1,
            ),
        ]
    )
    wout = jnp.stack([out_weight[:, :half], out_weight[:, half:]])
    parts = (norm_gain, conv_weight.reshape(-1), conv_bias, gate_norm)
    sizes = [part.size for part in parts]
    total = sum(sizes)
    srows = -(-total // 1024) * 8
    small = jnp.pad(jnp.concatenate(parts), (0, srows * 128 - total)).reshape(srows, 128)
    gin, gout, gsmall = gather_all(win, wout, small, n)
    gflat = gsmall.reshape(n, srows * 128)
    cuts = [0]
    for size in sizes:
        cuts.append(cuts[-1] + size)
    norm_full = gflat[:, cuts[0] : cuts[1]].reshape(-1)
    conv_full = jnp.swapaxes(gflat[:, cuts[1] : cuts[2]].reshape(n, KCONV, -1), 0, 1)
    conv_full = conv_full.reshape(KCONV, chans)
    cbias_full = gflat[:, cuts[2] : cuts[3]].reshape(-1)
    gnorm_full = gflat[:, cuts[3] : cuts[4]].reshape(-1)
    w_x = gin[0].reshape(width, chans)
    w_z = gin[1].reshape(width, chans)
    w_o0 = gout[0].reshape(inner, half)
    w_o1 = gout[1].reshape(inner, half)

    x_in = tokens.astype(F32)
    rinv = lax.rsqrt(jnp.mean(x_in * x_in, -1, keepdims=True) + EPS)
    unit = x_in * rinv
    h16 = (unit * norm_full).astype(B16)
    xbc16 = dot("qd,de->qe", h16, w_x).astype(B16)
    zd = dot("qd,de->qe", h16, w_z)
    zval = zd[:, :inner]
    dt_raw = zd[:, inner : inner + HEADS]
    edge = passed_along(xbc16[piece - edge_rows :], "seq", 1)
    padded16 = jnp.concatenate([edge, xbc16], 0)
    pre = cbias_full + conv_full[0] * padded16[0:piece]
    for k in range(1, KCONV):
        pre = pre + conv_full[k] * padded16[k : k + piece]
    xconv = jax.nn.silu(pre)
    xs16 = xconv[:, :inner].astype(B16).reshape(piece, HEADS, HEAD)
    bm16 = xconv[:, inner : inner + STATE].astype(B16)
    cm16 = xconv[:, inner + STATE :].astype(B16)
    shifted = dt_raw + dt_bias
    dth = jax.nn.softplus(shifted).T
    rate = -jnp.exp(a_log)
    lower = jnp.arange(piece)[:, None] >= jnp.arange(piece)[None, :]
    ones = lower.astype(F32)
    highest = lax.Precision.HIGHEST
    cumh = jnp.einsum("hu,tu->ht", dth * rate[:, None], ones, precision=highest)
    seg = jnp.where(lower, cumh[:, :, None] - cumh[:, None, :], -1e30)
    lmat = jnp.exp(seg)
    gram = dot("tn,un->tu", cm16, bm16)
    w16 = (gram[None] * lmat * dth[:, None, :]).astype(B16)
    y_diag = dot("htu,uhp->thp", w16, xs16)
    endc = cumh[:, -1]
    ewt = jnp.exp(endc[:, None] - cumh)
    factor = ewt * dth
    bw16 = (bm16[None] * factor[..., None]).astype(B16)
    s_loc = dot("hun,uhp->hpn", bw16, xs16)
    decay = jnp.exp(endc)
    s_in = carry_states(decay, s_loc, False)
    s_in16 = s_in.astype(B16)
    ecum = jnp.exp(cumh)
    ce16 = (cm16[None] * ecum[..., None]).astype(B16)
    y_off = dot("htn,hpn->thp", ce16, s_in16)
    xsf = xs16.astype(F32)
    yval = (y_diag + y_off + skip[:, None] * xsf).reshape(piece, inner)
    gate_act = jax.nn.silu(zval)
    gated = yval * gate_act
    grinv = lax.rsqrt(jnp.mean(gated * gated, -1, keepdims=True) + EPS)
    gunit = gated * grinv
    n16 = (gunit * gnorm_full).astype(B16)
    branch = jnp.concatenate([dot("qi,id->qd", n16, w_o0), dot("qi,id->qd", n16, w_o1)], -1)
    mixed = (x_in + branch).astype(B16)
    cot0 = cotangent[:, :half]
    cot1 = cotangent[:, half:]
    g_wout = jnp.stack(
        [dot("qi,qd->id", n16, cot0).astype(B16), dot("qi,qd->id", n16, cot1).astype(B16)]
    )
    dnorm = dot("qd,id->qi", cot0, w_o0) + dot("qd,id->qi", cot1, w_o1)
    g_gnorm = jnp.sum(dnorm * gunit, 0)
    dscaled = dnorm * gnorm_full
    dgated = grinv * (dscaled - gunit * jnp.mean(dscaled * gunit, -1, keepdims=True))
    dy16 = (dgated * gate_act).astype(B16).reshape(piece, HEADS, HEAD)
    dz = dgated * yval * silu_slope(zval)
    dyf = dy16.astype(F32)
    g_skip = jnp.sum(dyf * xsf, (0, 2))
    dxs = skip[:, None] * dyf
    dce = dot("thp,hpn->htn", dy16, s_in16)
    ds_loc_in = dot("htn,thp->hpn", ce16, dy16)
    dcm = jnp.sum(dce * ecum[..., None], 0)
    dcum = jnp.sum(dce * cm16[None] * ecum[..., None], -1)
    ds_out = carry_states(decay, ds_loc_in, True)
    dsl16 = ds_out.astype(B16)
    dend = jnp.sum(ds_out * s_in, (1, 2)) * decay
    dbw = dot("hpn,uhp->hun", dsl16, xs16)
    dxs = dxs + dot("hun,hpn->uhp", bw16, dsl16)
    dbm = jnp.sum(dbw * factor[..., None], 0)
    dfactor = jnp.sum(dbw * bm16[None], -1)
    ddt = dfactor * ewt
    dlog = dfactor * factor
    dend = dend + jnp.sum(dlog, -1)
    dcum = dcum - dlog
    dwmat = dot("thp,uhp->htu", dy16, xs16)
    dxs = dxs + dot("htu,thp->uhp", w16, dy16)
    dlmat = dwmat * gram[None] * dth[:, None, :]
    dg16 = jnp.sum(dwmat * lmat * dth[:, None, :], 0).astype(B16)
    ddt = ddt + jnp.sum(dwmat * gram[None] * lmat, 1)
    dseg = dlmat * lmat
    dcum = dcum + jnp.sum(dseg, 2) - jnp.sum(dseg, 1)
    dcm = dcm + dot("tu,un->tn", dg16, bm16)
    dbm = dbm + dot("tu,tn->un", dg16, cm16)
    dcum = dcum + jnp.pad(dend[:, None], ((0, 0), (piece - 1, 0)))
    dda = jnp.einsum("ht,tu->hu", dcum, ones, precision=highest)
    ddt = ddt + dda * rate[:, None]
    g_alog = jnp.sum(dda * dth, 1) * rate
    draw = ddt.T * jax.nn.sigmoid(shifted)
    g_dtb = jnp.sum(draw, 0)
    dxconv = jnp.concatenate([dxs.reshape(piece, inner), dbm, dcm], -1)
    dpre = dxconv * silu_slope(pre)
    g_cbias = jnp.sum(dpre, 0)
    g_conv = jnp.stack([jnp.sum(dpre * padded16[k : k + piece], 0) for k in range(KCONV)])
    dpadded = jnp.pad(conv_full[0] * dpre, ((0, edge_rows), (0, 0)))
    for k in range(1, KCONV):
        dpadded = dpadded + jnp.pad(conv_full[k] * dpre, ((k, edge_rows - k), (0, 0)))
    returned = passed_along(dpadded[:edge_rows], "seq", -1)
    dxbc = dpadded[edge_rows:] + jnp.pad(returned, ((piece - edge_rows, 0), (0, 0)))
    dxbc16 = dxbc.astype(B16)
    dzd16 = jnp.concatenate([dz, draw, jnp.zeros((piece, spare), F32)], -1).astype(B16)
    g_win = jnp.stack(
        [dot("qd,qe->de", h16, dxbc16).astype(B16), dot("qd,qe->de", h16, dzd16).astype(B16)]
    )
    dhid = dot("qe,de->qd", dxbc16, w_x) + dot("qe,de->qd", dzd16, w_z)
    g_norm = jnp.sum(dhid * unit, 0)
    dunit = dhid * norm_full
    dx_in = cotangent.astype(F32) + rinv * (
        dunit - unit * jnp.mean(dunit * unit, -1, keepdims=True)
    )
    grad_tokens = dx_in.astype(B16)

    psmall = jnp.concatenate(
        [
            g_norm.reshape(n, -1),
            jnp.swapaxes(g_conv.reshape(KCONV, n, -1), 0, 1).reshape(n, -1),
            g_cbias.reshape(n, -1),
            g_gnorm.reshape(n, -1),
            jnp.zeros((n, srows * 128 - total), F32),
        ],
        1,
    ).reshape(n, srows, 128)
    phead = jnp.pad(jnp.stack([g_dtb, g_alog, g_skip]), ((0, 5), (0, 128 - HEADS)))
    oin, oout, osmall, ohead = reduce_all(
        g_win.reshape(2, n, rows, chans), g_wout.reshape(2, n, orows, half), psmall, phead, n, ny
    )
    flat = osmall.reshape(-1)
    return (
        mixed[None],
        grad_tokens[None],
        flat[cuts[0] : cuts[1]],
        jnp.concatenate([oin[1, :, :inner], oin[0], oin[1, :, inner : inner + HEADS]], 1),
        flat[cuts[1] : cuts[2]].reshape(KCONV, -1),
        flat[cuts[2] : cuts[3]],
        ohead[0, :HEADS],
        ohead[1, :HEADS],
        ohead[2, :HEADS],
        flat[cuts[3] : cuts[4]],
        jnp.concatenate([oout[0], oout[1]], 1),
    )


def solution(mesh):
    placed = (
        P("dp", "seq", None),
        P("dp"),
        P("dp", None),
        P(None, "dp"),
        P("dp"),
        P(),
        P(),
        P(),
        P("dp"),
        P("dp", None),
        P("dp", "seq", None),
    )
    return jax.shard_map(
        body,
        mesh=mesh,
        in_specs=placed,
        out_specs=(
            P("dp", "seq", None),
            P("dp", "seq", None),
            P("dp"),
            P("dp", None),
            P(None, "dp"),
            P("dp"),
            P(),
            P(),
            P(),
            P("dp"),
            P("dp", None),
        ),
        check_vma=False,
    )
```

time: 525 us -> 284 us (0.54)
  blocking collectives: 158 us -> 0 us
  waiting for transfers between devices: 154 us -> 18.4 us
  Pallas kernels: 0 us -> 121 us
  other arithmetic: 57.2 us -> 33.9 us
  between operations: 19.1 us -> 2.05 us
  local copies, waits for them, and re-layouts: 51.9 us -> 37.1 us
  starting transfers between devices: 30.6 us -> 21.3 us
    pallas_call x0 -> x2, Pallas kernels: none -> 121 us  [the longest x1 67.6 us: reduce_all(): pl.pallas_call(functools.partial(reduce_kernel, n, ny), out_shape=(jax.Sh...]
    unnamed x2 -> x0, blocking collectives: 75.5 us -> none
    unnamed x7 -> x0, waiting for transfers between devices: 66.1 us -> none
    psum x2 -> x0, blocking collectives: 49.1 us -> none  [the longest x1 43.5 us: body(): head_sums = lax.psum((g_dtb, g_alog, g_skip), ('dp', 'seq'))]
    all_gather x1 -> x0, blocking collectives: 32.9 us -> none  [body(): lax.all_gather(conv_weight, 'dp', axis=1, tiled=True)]
    psum x1 -> x0, waiting for transfers between devices: 28 us -> none  [body(): lax.psum(owned[1].astype(jnp.bfloat16), 'seq').astype(jnp.float32)]
    reduce_scatter x2 -> x0, waiting for transfers between devices: 24.4 us -> none  [the longest x1 24.4 us: body(): lax.psum_scatter(g_win.astype(jnp.bfloat16), 'dp', scatter_dimension=0, t...]
    all_gather x2 -> x0, waiting for transfers between devices: 11.5 us -> none  [the longest x1 11.5 us: gather_weights(): lax.all_gather(in_weight, 'dp', axis=0, tiled=True)]
  transfers between devices with their start and end apart: 14 -> 8, of which waited for: 8 -> 3; matrix products, arithmetic and copies ran while one was open for 27% -> 8% of each run, Pallas kernels for 0% -> 0%
where the time goes in v1:
time: 284 us; the launch traced here: 283 us
  Pallas kernels  121 us (43%)
  matrix products  49.6 us (17%)
  local copies, waits for them, and re-layouts  37.1 us (13%)
  other arithmetic  33.9 us (12%)
  starting transfers between devices  21.3 us (8%)
  waiting for transfers between devices  18.4 us (6%)
    pallas_call x1, Pallas kernels, reduce_all(): pl.pallas_call(functools.partial(reduce_kernel, n, ny), out_shape=(jax.Sh...  67.6 us
    pallas_call x1, Pallas kernels, gather_all(): pl.pallas_call(functools.partial(gather_kernel, n), out_shape=(jax.ShapeD...  52.9 us
    dot_general x24, matrix products, dot(): return jnp.einsum(spec, left, right, preferred_element_type=F32)  49.1 us
    ppermute x8, starting transfers between devices, passed_along(): return lax.ppermute(block, axis, route)  21.3 us
    ppermute x8, waiting for transfers between devices, passed_along(): return lax.ppermute(block, axis, route)  18.4 us
    reduce_sum x1, other arithmetic, body(): jnp.sum(dpre * padded16[k:k + piece], 0)  6.52 us
    unnamed x181, local copies, waits for them, and re-layouts  5.81 us
  transfers between devices with their start and end apart: 8, of which 3 were waited for; matrix products, arithmetic and copies ran while one was open for 8% of the time, Pallas kernels for 0%

profile of v1, /device:TPU:0, one launch (start us, length us, event | category | flops | bytes accessed | tf_op | source)
XLA Modules:
  0.0 282.9 jit_solution(13229986070696904755)
XLA Ops:
  3.3 52.9 %gather_weights.1 = (bf16[2,8,96,1792]{3,2,1,0:T(8,128)(2,1)S(1)}, bf16[2,8,192,384]{3,2,1,0:T(8,128)(2,1)S(1)}, f32[8,16,128]{2,1,0:T(8,128)S(1)}) custom-call(bf16[2,96,1792]{2,1,0:T(8,128)(2,1)S(1)} %pad_maximum_fusion.4.win, bf16[2,192,384]{2,1,0:T(8,128)(2,1)S(1)} %pad_maximum_fusion.6.wout, f32[16,128]{1,0:T(8,128)S(1)} %pad_bitcast_fusion.small), custom_call_target="tpu_custom_call" | custom-call | tf_op jit(solution)/shard_map/gather_weights/pallas_call | solution.py:122
  56.2 2.4 copy-done
  58.7 3.0 %fusion.89 = (bf16[1,8,96,1792]{3,2,1,0:T(8,128)(2,1)S(1)}, bf16[1,8,96,1792]{3,2,1,0:T(8,128)(2,1)S(1)}) fusion(bf16[2,8,96,1792]{3,2,1,0:T(8,128)(2,1)} %copy-done), kind=kLoop, calls=%fused_computation.191 | loop fusion | bytes 11010048 | tf_op jit(solution)/shard_map/slice | solution.py:460
  70.4 4.1 %multiply_convert_fusion.9 = bf16[256,1792]{1,0:T(8,128)(2,1)S(1)} fusion(bf16[256,1792]{1,0:T(8,128)(2,1)} %copy-done.15, f32[1792]{0:T(1024)S(1)} %mul.437, bf16[3,1792]{1,0:T(4,128)(2,1)S(1)} %collective-permute-done, f32[1792]{0:T(1024)S(1)} %mul.434, f32[1792]{0:T(1024)S(1)} %mul.431, f32[1792]{0:T(1024)S(1)} %mul.422, f32[1792]{0:T(1024)S(1)} %add.170), kind=kLoop, calls=%fused_computation.48 | loop fusion | flops 11927552 | bytes 1881600 | tf_op jit(solution)/shard_map/convert.6
  80.0 3.2 %collective-permute-start.1 = (bf16[24,64,128]{2,1,0:T(8,128)(2,1)S(1)}, bf16[24,64,128]{2,1,0:T(8,128)(2,1)S(1)}, u32[]{:S(2)}, u32[]{:S(2)}) collective-permute-start(bf16[24,64,128]{2,1,0:T(8,128)(2,1)S(1)} %get-tuple-element.76), channel_id=1, source_target_pairs={{0,1},{1,2},{2,3},{4,5},{5,6},{6,7},{8,9},{9,10},{10,11},{12,13},{... | collective-permute-start | bytes 1179656 | tf_op jit(solution)/shard_map/ppermute | solution.py:384
  84.7 5.7 %collective-permute-start.2 = (bf16[24,64,128]{2,1,0:T(8,128)(2,1)S(1)}, bf16[24,64,128]{2,1,0:T(8,128)(2,1)S(1)}, u32[]{:S(2)}, u32[]{:S(2)}) collective-permute-start(bf16[24,64,128]{2,1,0:T(8,128)(2,1)S(1)} %add_convert_fusion.4), channel_id=1, source_target_pairs={{0,1},{1,2},{2,3},{4,5},{5,6},{6,7},{8,9},{9,10},{10,11},{12,13},{... | collective-permute-start | bytes 1179656 | tf_op jit(solution)/shard_map/ppermute | solution.py:384
  96.7 4.6 %collective-permute-start.3 = (bf16[24,64,128]{2,1,0:T(8,128)(2,1)S(1)}, bf16[24,64,128]{2,1,0:T(8,128)(2,1)S(1)}, u32[]{:S(2)}, u32[]{:S(2)}) collective-permute-start(bf16[24,64,128]{2,1,0:T(8,128)(2,1)S(1)} %add_convert_fusion.3), channel_id=1, source_target_pairs={{0,1},{1,2},{2,3},{4,5},{5,6},{6,7},{8,9},{9,10},{10,11},{12,13},{... | collective-permute-start | bytes 1179656 | tf_op jit(solution)/shard_map/ppermute | solution.py:384
  104.7 3.2 %copy.156 = f32[256,1536]{1,0:T(8,128)} copy(f32[256,1536]{0,1:T(8,128)} %bitcast.162) | data formatting | bytes 3145728 | tf_op jit(solution)/shard_map/reshape | solution.py:505
  111.8 3.1 %multiply_reduce_fusion.6 = (f32[1536]{0:T(1024)}, bf16[256,1536]{1,0:T(8,128)(2,1)}, bf16[256,1536]{1,0:T(8,128)(2,1)}, bf16[256,1536]{1,0:T(8,128)(2,1)S(1)}) fusion(bf16[256,1792]{1,0:T(8,128)(2,1)S(1)} %copy-done.12, f32[256,1792]{1,0:T(8,128)S(1)} %copy-done.3, f32[256]{0:T(256)S(1)} %broadcast_multiply_fusion.4, f32[256,1536]{1,0:T(8,128)S(1)} %get-tuple-element.52, ...), kind=kLoop, calls=%fused_computation.53 | loop fusion | flops 9435648 | bytes 9451520 | tf_op jit(solution)/shard_map/reduce_sum | solution.py:525
  116.4 2.8 add_convert_fusion.2
  119.2 5.4 %fusion.1 = (f32[24,256]{1,0:T(8,128)}, f32[24,256]{1,0:T(8,128)}, f32[24,256]{1,0:T(8,128)}, bf16[256,256]{1,0:T(8,128)(2,1)S(1)}) fusion(f32[24,256]{1,0:T(8,128)S(1)} %copy-done.64, f32[24,256]{1,0:T(8,128)S(1)} %copy-done.52, f32[256,256]{1,0:T(8,128)S(1)} %copy-done.37, pred[256,256]{1,0:T(8,128)(4,1)S(1)} %copy-done.58, ...), kind=kOutput, calls=%fused_computation.7 | convolution fusion | flops 220116992 | bytes 2154496 | tf_op jit(solution)/shard_map/thp,uhp->htu/dot_general | solution.py:401
  133.1 2.8 multiply_reduce_fusion.4
  145.2 5.0 %collective-permute-done.5 = bf16[24,64,128]{2,1,0:T(8,128)(2,1)S(1)} collective-permute-done((bf16[24,64,128]{2,1,0:T(8,128)(2,1)S(1)}, bf16[24,64,128]{2,1,0:T(8,128)(2,1)S(1)}, u32[]{:S(2)}, u32[]{:S(2)}) %collective-permute-start.5) | collective-permute-done | bytes 393248 | tf_op jit(solution)/shard_map/ppermute | solution.py:384
  153.8 6.5 %collective-permute-done.6 = bf16[24,64,128]{2,1,0:T(8,128)(2,1)S(1)} collective-permute-done((bf16[24,64,128]{2,1,0:T(8,128)(2,1)S(1)}, bf16[24,64,128]{2,1,0:T(8,128)(2,1)S(1)}, u32[]{:S(2)}, u32[]{:S(2)}) %collective-permute-start.6) | collective-permute-done | bytes 393248 | tf_op jit(solution)/shard_map/ppermute | solution.py:384
  162.0 3.1 %copy.166 = f32[256,1536]{1,0:T(8,128)} copy(f32[256,1536]{0,1:T(8,128)} %bitcast.161) | data formatting | bytes 3145728 | tf_op jit(solution)/shard_map/reshape | solution.py:557
  165.0 2.6 multiply_reduce_fusion.5
  169.6 6.5 %fusion.13 = (f32[1792]{0:T(1024)S(1)}, f32[1792]{0:T(1024)S(1)}, f32[1792]{0:T(1024)S(1)}, f32[1792]{0:T(1024)S(1)}, f32[1792]{0:T(1024)S(1)}, /*index=5*/f32[256,1792]{1,0:T(8,128)S(1)}) fusion(bf16[256,1792]{1,0:T(8,128)(2,1)} %copy-done.15, bf16[3,1792]{1,0:T(4,128)(2,1)} %copy-done.60, f32[1792]{0:T(1024)} %copy-done.47, f32[1792]{0:T(1024)} %copy-done.45, ...), kind=kLoop, calls=%fused_computation.41 | loop fusion | flops 22011136 | bytes 4669952 | tf_op jit(solution)/shard_map/reduce_sum | solution.py:560
  182.0 4.0 %fusion.93 = f32[256,768]{1,0:T(8,128)} fusion(bf16[256,1792]{1,0:T(8,128)(2,1)} %concatenate.43, bf16[768,1792]{1,0:T(8,128)(2,1)} %bitcast.156), kind=kOutput, calls=%fused_computation.195 | convolution fusion | flops 704643072 | bytes 4456448 | tf_op jit(solution)/shard_map/qe,de->qd/dot_general | solution.py:401
  186.0 2.6 convolution_convert_fusion
  191.0 6.8 %collective-permute-done.7 = f32[3,1792]{1,0:T(4,128)S(1)} collective-permute-done((f32[3,1792]{1,0:T(4,128)S(1)}, f32[3,1792]{1,0:T(4,128)S(1)}, u32[]{:S(2)}, u32[]{:S(2)}) %collective-permute-start.7) | collective-permute-done | bytes 21536 | tf_op jit(solution)/shard_map/ppermute | solution.py:384
  197.7 4.4 %fusion.41 = (f32[768]{0:T(1024)S(1)}, f32[256]{0:T(256)S(1)}, f32[256,768]{1,0:T(8,128)}) fusion(bf16[1,256,768]{2,1,0:T(8,128)(2,1)S(1)} %copy-done.5, f32[256]{0:T(256)S(1)} %add_rsqrt_fusion.1, f32[768]{0:T(1024)S(1)} %mul.427, f32[256,768]{1,0:T(8,128)} %fusion.93, bf16[768,1792]{1,0:T(8,128)(2,1)} %bitcast.180, f32[259,1792]{1,0:T(8,128)} %pad_add_fusion, ...), kind=kOutput, calls=%fused_computation.99 | convolution fusion | flops 707132416 | bytes 6583296 | tf_op jit(solution)/shard_map/qe,de->qd/dot_general | solution.py:401
  202.3 2.7 convolution_convert_fusion.1
  205.0 2.9 %pad_maximum_fusion.pin = bf16[2,8,96,1792]{3,2,1,0:T(8,128)(2,1)} fusion(bf16[1,8,96,1792]{3,2,1,0:T(8,128)(2,1)S(1)} %bitcast.154, bf16[1,8,96,1792]{3,2,1,0:T(8,128)(2,1)S(1)} %bitcast.181), kind=kLoop, calls=%fused_computation.5 | loop fusion | flops 2752512 | bytes 11010048 | tf_op jit(solution)/shard_map/stack | solution.py:568
  207.9 67.6 %reduce_gradients.1 = (f32[2,96,1792]{2,1,0:T(8,128)S(1)}, f32[2,192,384]{2,1,0:T(8,128)S(1)}, f32[16,128]{1,0:T(8,128)S(1)}, f32[8,128]{1,0:T(8,128)S(1)}) custom-call(bf16[2,8,96,1792]{3,2,1,0:T(8,128)(2,1)} %pad_maximum_fusion.pin, bf16[2,8,192,384]{3,2,1,0:T(8,128)(2,1)S(1)} %pad_maximum_fusion.1.pout, f32[8,16,128]{2,1,0:T(8,128)S(1)} %bitcast.148, ...), custom_call_target="tpu_custom_call" | custom-call | tf_op jit(solution)/shard_map/reduce_gradients/pallas_call | solution.py:335
  (305 shorter events, 73.1 us)
Async XLA Ops:
  58.6 11.2 %copy-start.42 = (f32[1,8,16,128]{3,1,2,0:T(8,128)}, f32[1,8,16,128]{3,1,2,0:T(8,128)S(1)}, u32[]{:S(2)}) copy-start(f32[1,8,16,128]{3,1,2,0:T(8,128)S(1)} %copy.185) | copy-start | bytes 196612
  62.9 7.4 %collective-permute-start = (bf16[3,1792]{1,0:T(4,128)(2,1)S(1)}, bf16[3,1792]{1,0:T(4,128)(2,1)S(1)}, u32[]{:S(2)}, u32[]{:S(2)}) collective-permute-start(bf16[3,1792]{1,0:T(4,128)(2,1)S(1)} %slice.190), channel_id=1, source_target_pairs={{0,1},{1,2},{2,3},{4,5},{5,6},{6,7},{8,9},{9,10},{10,11},{12,13},{... | collective-permute-start | bytes 32264 | tf_op jit(solution)/shard_map/ppermute | solution.py:384
  69.2 9.1 %copy-start.39 = (f32[24,256]{1,0:T(8,128)}, f32[24,256]{1,0:T(8,128)S(1)}, u32[]{:S(2)}) copy-start(f32[24,256]{1,0:T(8,128)S(1)} %get-tuple-element.70) | copy-start | bytes 73732
  69.7 8.5 %copy-start.82 = (f32[24]{0:T(128)}, f32[24]{0:T(128)S(1)}, u32[]{:S(2)}) copy-start(f32[24]{0:T(128)S(1)} %get-tuple-element.75) | copy-start | bytes 292
  80.0 4.5 %collective-permute-start.1 = (bf16[24,64,128]{2,1,0:T(8,128)(2,1)S(1)}, bf16[24,64,128]{2,1,0:T(8,128)(2,1)S(1)}, u32[]{:S(2)}, u32[]{:S(2)}) collective-permute-start(bf16[24,64,128]{2,1,0:T(8,128)(2,1)S(1)} %get-tuple-element.76), channel_id=1, source_target_pairs={{0,1},{1,2},{2,3},{4,5},{5,6},{6,7},{8,9},{9,10},{10,11},{12,13},{... | collective-permute-start | bytes 1179656 | tf_op jit(solution)/shard_map/ppermute | solution.py:384
  83.3 7.2 %copy-start.17 = (bf16[1,256,768]{2,1,0:T(8,128)(2,1)S(1)}, bf16[1,256,768]{2,1,0:T(8,128)(2,1)}, u32[]{:S(2)}) copy-start(bf16[1,256,768]{2,1,0:T(8,128)(2,1)} %param.21) | copy-start | bytes 1179652
  84.5 7.8 %copy-start.9 = (bf16[1,8,192,384]{3,2,1,0:T(8,128)(2,1)}, bf16[1,8,192,384]{3,2,1,0:T(8,128)(2,1)S(1)}, u32[]{:S(2)}) copy-start(bf16[1,8,192,384]{3,2,1,0:T(8,128)(2,1)S(1)} %get-tuple-element.56) | copy-start | bytes 3538948
  84.7 11.0 %collective-permute-start.2 = (bf16[24,64,128]{2,1,0:T(8,128)(2,1)S(1)}, bf16[24,64,128]{2,1,0:T(8,128)(2,1)S(1)}, u32[]{:S(2)}, u32[]{:S(2)}) collective-permute-start(bf16[24,64,128]{2,1,0:T(8,128)(2,1)S(1)} %add_convert_fusion.4), channel_id=1, source_target_pairs={{0,1},{1,2},{2,3},{4,5},{5,6},{6,7},{8,9},{9,10},{10,11},{12,13},{... | collective-permute-start | bytes 1179656 | tf_op jit(solution)/shard_map/ppermute | solution.py:384
  92.3 9.0 %copy-start.18 = (bf16[256,1536]{0,1:T(8,128)(2,1)S(1)}, bf16[256,1536]{0,1:T(8,128)(2,1)}, u32[]{:S(2)}) copy-start(bf16[256,1536]{0,1:T(8,128)(2,1)} %copy.150) | copy-start | bytes 2359300
  94.6 8.5 %copy-start.32 = (f32[256,128]{0,1:T(8,128)}, f32[256,128]{0,1:T(8,128)S(1)}, u32[]{:S(2)}) copy-start(f32[256,128]{0,1:T(8,128)S(1)} %copy.154) | copy-start | bytes 393220
  95.7 7.3 %copy-start.36 = (f32[256,256]{1,0:T(8,128)}, f32[256,256]{1,0:T(8,128)S(1)}, u32[]{:S(2)}) copy-start(f32[256,256]{1,0:T(8,128)S(1)} %fusion.68) | copy-start | bytes 786436
  96.7 6.4 %collective-permute-start.3 = (bf16[24,64,128]{2,1,0:T(8,128)(2,1)S(1)}, bf16[24,64,128]{2,1,0:T(8,128)(2,1)S(1)}, u32[]{:S(2)}, u32[]{:S(2)}) collective-permute-start(bf16[24,64,128]{2,1,0:T(8,128)(2,1)S(1)} %add_convert_fusion.3), channel_id=1, source_target_pairs={{0,1},{1,2},{2,3},{4,5},{5,6},{6,7},{8,9},{9,10},{10,11},{12,13},{... | collective-permute-start | bytes 1179656 | tf_op jit(solution)/shard_map/ppermute | solution.py:384
  130.4 10.4 %collective-permute-start.4 = (bf16[24,64,128]{2,1,0:T(8,128)(2,1)}, bf16[24,64,128]{2,1,0:T(8,128)(2,1)}, u32[]{:S(2)}, u32[]{:S(2)}) collective-permute-start(bf16[24,64,128]{2,1,0:T(8,128)(2,1)} %get-tuple-element.79), channel_id=1, source_target_pairs={{1,0},{2,1},{3,2},{5,4},{6,5},{7,6},{9,8},{10,9},{11,10},{13,12},{... | collective-permute-start | bytes 1179656 | tf_op jit(solution)/shard_map/ppermute | solution.py:384
  142.0 8.2 %collective-permute-start.5 = (bf16[24,64,128]{2,1,0:T(8,128)(2,1)S(1)}, bf16[24,64,128]{2,1,0:T(8,128)(2,1)S(1)}, u32[]{:S(2)}, u32[]{:S(2)}) collective-permute-start(bf16[24,64,128]{2,1,0:T(8,128)(2,1)S(1)} %add_convert_fusion.1), channel_id=1, source_target_pairs={{1,0},{2,1},{3,2},{5,4},{6,5},{7,6},{9,8},{10,9},{11,10},{13,12},{... | collective-permute-start | bytes 1179656 | tf_op jit(solution)/shard_map/ppermute | solution.py:384
  144.3 7.6 %copy-start.21 = (bf16[256,1536]{0,1:T(8,128)(2,1)S(1)}, bf16[256,1536]{0,1:T(8,128)(2,1)}, u32[]{:S(2)}) copy-start(bf16[256,1536]{0,1:T(8,128)(2,1)} %copy-done.20) | copy-start | bytes 2359300
  144.3 7.6 %copy-start.38 = (f32[256,256]{1,0:T(8,128)S(1)}, f32[256,256]{1,0:T(8,128)}, u32[]{:S(2)}) copy-start(f32[256,256]{1,0:T(8,128)} %copy-done.36) | copy-start | bytes 786436
  144.3 7.6 %copy-start.53 = (f32[24,256]{1,0:T(8,128)S(1)}, f32[24,256]{1,0:T(8,128)}, u32[]{:S(2)}) copy-start(f32[24,256]{1,0:T(8,128)} %copy-done.50) | copy-start | bytes 73732
  144.3 7.6 %copy-start.59 = (pred[256,256]{1,0:T(8,128)(4,1)S(1)}, pred[256,256]{1,0:T(8,128)(4,1)}, u32[]{:S(2)}) copy-start(pred[256,256]{1,0:T(8,128)(4,1)} %iota_compare_fusion) | copy-start | bytes 196612
  144.3 7.6 %copy-start.65 = (f32[24,256]{1,0:T(8,128)S(1)}, f32[24,256]{1,0:T(8,128)}, u32[]{:S(2)}) copy-start(f32[24,256]{1,0:T(8,128)} %copy-done.62) | copy-start | bytes 73732
  150.4 9.9 %copy-start.40 = (f32[24,256]{1,0:T(8,128)S(1)}, f32[24,256]{1,0:T(8,128)}, u32[]{:S(2)}) copy-start(f32[24,256]{1,0:T(8,128)} %copy-done.39) | copy-start | bytes 73732
  150.4 9.9 %copy-start.73 = (f32[24]{0:T(128)S(1)}, f32[24]{0:T(128)}, u32[]{:S(2)}) copy-start(f32[24]{0:T(128)} %param.18) | copy-start | bytes 292
  150.4 9.8 %collective-permute-start.6 = (bf16[24,64,128]{2,1,0:T(8,128)(2,1)S(1)}, bf16[24,64,128]{2,1,0:T(8,128)(2,1)S(1)}, u32[]{:S(2)}, u32[]{:S(2)}) collective-permute-start(bf16[24,64,128]{2,1,0:T(8,128)(2,1)S(1)} %add_convert_fusion), channel_id=1, source_target_pairs={{1,0},{2,1},{3,2},{5,4},{6,5},{7,6},{9,8},{10,9},{11,10},{13,12},{... | collective-permute-start | bytes 1179656 | tf_op jit(solution)/shard_map/ppermute | solution.py:384
  189.2 8.6 %collective-permute-start.7 = (f32[3,1792]{1,0:T(4,128)S(1)}, f32[3,1792]{1,0:T(4,128)S(1)}, u32[]{:S(2)}, u32[]{:S(2)}) collective-permute-start(f32[3,1792]{1,0:T(4,128)S(1)} %pad_add_fusion.1), channel_id=1, source_target_pairs={{1,0},{2,1},{3,2},{5,4},{6,5},{7,6},{9,8},{10,9},{11,10},{13,12},{... | collective-permute-start | bytes 64520 | tf_op jit(solution)/shard_map/ppermute | solution.py:384
  191.0 11.2 %copy-start.61 = (f32[8,192]{1,0:T(8,128)S(1)}, f32[8,192]{1,0:T(8,128)}, u32[]{:S(2)}) copy-start(f32[8,192]{1,0:T(8,128)} %reshape.186) | copy-start | bytes 18436
  (75 other events, 247.6 us)

commit v2 on v1

--- a/solution.py
+++ b/solution.py
@@ -390,15 +390,271 @@
 
 
 def carry_states(decay, local, reverse):
-    moved = jnp.zeros_like(local)
+    moved = jnp.zeros_like(local, dtype=B16)
     for step in range(lax.axis_size("seq") - 1):
-        total = (decay[:, None, None] * moved.astype(F32) + local).astype(B16)
+        total = (decay * moved.astype(F32) + local).astype(B16)
         moved = passed_along(total, "seq", -1 if reverse else 1)
-    return moved.astype(F32)
-
-
-def dot(spec, left, right):
-    return jnp.einsum(spec, left, right, preferred_element_type=F32)
+    return moved
+
+
+def mm(left, right, dims=((1,), (0,)), precision=None):
+    return lax.dot_general(
+        left, right, (dims, ((), ())), precision=precision, preferred_element_type=F32
+    )
+
+
+NT = ((1,), (1,))
+TN = ((0,), (0,))
+HIGHEST = lax.Precision.HIGHEST
+
+
+def head_map():
+    lane = lax.broadcasted_iota(jnp.int32, (128, HEADS * HEAD), 1) // HEAD
+    return (lane == lax.broadcasted_iota(jnp.int32, (128, HEADS * HEAD), 0)).astype(B16)
+
+
+def split(value):
+    high = value.astype(B16)
+    return high, (value - high.astype(F32)).astype(B16)
+
+
+def spread(value):
+    high, rest = split(value)
+    place = head_map()
+    return mm(high, place) + mm(rest, place)
+
+
+def gathered(value):
+    high, rest = split(value)
+    place = head_map()
+    return mm(high, place, NT) + mm(rest, place, NT)
+
+
+def triangle(piece):
+    row = lax.broadcasted_iota(jnp.int32, (piece, piece), 0)
+    return row >= lax.broadcasted_iota(jnp.int32, (piece, piece), 1)
+
+
+def pair_masks(shape):
+    first = lax.broadcasted_iota(jnp.int32, shape, 1) < HEAD
+    return first, jnp.logical_not(first)
+
+
+def local_call(kernel, outs, *args):
+    vmem = pl.BlockSpec(memory_space=pltpu.VMEM)
+    shapes = tuple(jax.ShapeDtypeStruct(shape, dtype) for shape, dtype in outs)
+    moved = sum(a.size * a.dtype.itemsize for a in args)
+    return pl.pallas_call(
+        kernel,
+        out_shape=shapes,
+        in_specs=[vmem] * len(args),
+        out_specs=(vmem,) * len(outs),
+        compiler_params=pltpu.CompilerParams(vmem_limit_bytes=44 * 2**20),
+        cost_estimate=pl.CostEstimate(
+            flops=10**9 * 5, bytes_accessed=moved, transcendentals=10**6
+        ),
+        name=kernel.__name__,
+    )(*args)
+
+
+def project(tok, norm, gin, conv, cbias, dtb, rate, h, xbc, pre, z, shift, dt, cum, xs, bm, cm, sloc, decay):
+    piece = h.shape[0]
+    inner = HEADS * HEAD
+    x = tok[...].astype(F32)
+    rinv = lax.rsqrt(jnp.mean(x * x, -1, keepdims=True) + EPS)
+    h16 = (x * rinv * norm[...]).astype(B16)
+    h[...] = h16[8:]
+    padded16 = mm(h16, gin[0]).astype(B16)
+    xbc[...] = padded16
+    padded = padded16.astype(F32)
+    zd = mm(h16[8:], gin[1])
+    z[...] = zd[:, :inner]
+    p = cbias[...] + conv[0:1] * padded[5 : 5 + piece]
+    for k in range(1, KCONV):
+        p = p + conv[k : k + 1] * padded[5 + k : 5 + k + piece]
+    pre[...] = p
+    xconv = (p * jax.nn.sigmoid(p)).astype(B16)
+    xs16 = xconv[:, :inner]
+    b16 = xconv[:, inner : inner + STATE]
+    xs[...] = xs16
+    bm[...] = b16
+    cm[...] = xconv[:, inner + STATE :]
+    shifted = zd[:, inner : inner + 128] + dtb[...]
+    shift[...] = shifted
+    step = jnp.maximum(shifted, 0.0) + jnp.log1p(jnp.exp(-jnp.abs(shifted)))
+    dt[...] = step
+    total = mm(triangle(piece).astype(F32), step * rate[...], precision=HIGHEST)
+    cum[...] = total
+    endc = total[piece - 1 : piece]
+    xf = (xs16.astype(F32) * spread(jnp.exp(endc - total) * step)).astype(B16)
+    sloc[...] = mm(b16, xf, TN)
+    decay[...] = spread(jnp.broadcast_to(jnp.exp(endc), (8, 128)))
+
+
+def diagonal(xs, bm, cm, dt, cum, y):
+    piece = xs.shape[0]
+    gram = mm(cm[...], bm[...], NT)
+    lower = triangle(piece)
+    cumc = cum[...]
+    cumr = cumc.T
+    dtr = dt[...].T
+    masks = pair_masks((piece, 128))
+    zero = jnp.zeros((piece, 128), B16)
+    for j in range(HEADS // 2):
+        pair = xs[:, 128 * j : 128 * j + 128]
+        out = None
+        for i in range(2):
+            k = 2 * j + i
+            seg = jnp.where(lower, cumc[:, k : k + 1] - cumr[k : k + 1], -1e30)
+            w = (gram * jnp.exp(seg) * dtr[k : k + 1]).astype(B16)
+            part = mm(w, jnp.where(masks[i], pair, zero))
+            out = part if out is None else out + part
+        y[:, 128 * j : 128 * j + 128] = out
+
+
+def gate(tok, sin, ydiag, xs, cm, cum, z, skip, gnorm, gout, cot, mixed, normed, dy, dz, ggn, gsk, dsl, dcm, dcum):
+    half = tok.shape[1] // 2
+    ecx = spread(jnp.exp(cum[...]))
+    s16 = sin[...]
+    yoff = mm(cm[...], s16) * ecx
+    xsf = xs[...].astype(F32)
+    y = ydiag[...] + yoff + skip[...] * xsf
+    zv = z[...]
+    sig = jax.nn.sigmoid(zv)
+    act = zv * sig
+    gated = y * act
+    grinv = lax.rsqrt(jnp.mean(gated * gated, -1, keepdims=True) + EPS)
+    gunit = gated * grinv
+    n16 = (gunit * gnorm[...]).astype(B16)
+    normed[...] = n16
+    for i in range(2):
+        cols = slice(half * i, half * i + half)
+        mixed[:, cols] = (tok[:, cols].astype(F32) + mm(n16, gout[i])).astype(B16)
+    dn = mm(cot[:, :half], gout[0], NT) + mm(cot[:, half:], gout[1], NT)
+    ggn[...] = jnp.sum(dn * gunit, 0, keepdims=True)
+    ds = dn * gnorm[...]
+    dgated = grinv * (ds - gunit * jnp.mean(ds * gunit, -1, keepdims=True))
+    dy16 = (dgated * act).astype(B16)
+    dy[...] = dy16
+    dz[...] = (dgated * y * (sig * (1.0 + zv * (1.0 - sig)))).astype(B16)
+    dyf = dy16.astype(F32)
+    gsk[...] = jnp.sum(dyf * xsf, 0, keepdims=True)
+    dye = (dyf * ecx).astype(B16)
+    dsl[...] = mm(cm[...], dye, TN)
+    dcm[...] = mm(dye, s16, NT)
+    dcum[...] = gathered(dyf * yoff)
+
+
+def diagonal_back(xs, bm, cm, dt, cum, dy, normed, cot, dxs, ddt, dcum, dcm, dbm, gw, rows):
+    piece = xs.shape[0]
+    half = cot.shape[1] // 2
+    gw[0] = mm(normed[...], cot[:, :half], TN).astype(B16)
+    gw[1] = mm(normed[...], cot[:, half:], TN).astype(B16)
+    gram = mm(cm[...], bm[...], NT)
+    lower = triangle(piece)
+    cumc = cum[...]
+    cumr = cumc.T
+    dtr = dt[...].T
+    masks = pair_masks((piece, 128))
+    zero = jnp.zeros((piece, 128), B16)
+    lane = lax.broadcasted_iota(jnp.int32, (piece, 128), 1)
+    dcum[...] = jnp.zeros((piece, 128), F32)
+    rows[...] = jnp.zeros((128, piece), F32)
+    dg = jnp.zeros((piece, piece), F32)
+    for j in range(HEADS // 2):
+        cols = slice(128 * j, 128 * j + 128)
+        pair = xs[:, cols]
+        dpair = dy[:, cols]
+        out = None
+        for i in range(2):
+            k = 2 * j + i
+            seg = jnp.where(lower, cumc[:, k : k + 1] - cumr[k : k + 1], -1e30)
+            lmat = jnp.exp(seg)
+            dmask = jnp.where(masks[i], dpair, zero)
+            dw = mm(dmask, pair, NT)
+            row = dtr[k : k + 1]
+            w = (gram * lmat * row).astype(B16)
+            part = mm(w, dmask, TN)
+            out = part if out is None else out + part
+            q = dw * lmat
+            dg = dg + q * row
+            gl = q * gram
+            rows[k : k + 1, :] = jnp.sum(gl, 0, keepdims=True)
+            col = jnp.sum(gl * row, 1, keepdims=True)
+            dcum[...] = jnp.where(lane == k, col, dcum[...])
+        dxs[:, cols] = out
+    ddt[...] = rows[...].T
+    dcum[...] = dcum[...] - ddt[...] * dt[...]
+    dg16 = dg.astype(B16)
+    dcm[...] = mm(dg16, bm[...])
+    dbm[...] = mm(dg16, cm[...], TN)
+
+
+def state_back(dso, sin, decay, xs, bm, dt, cum, dy, dxsd, ddtq, dcumq, dcmq, dbmq, dcum3, dcm3, skip, pre, xbc, shift, rate, dpre, draw, gdtb, galog, gcb, gconv):
+    piece = xs.shape[0]
+    inner = HEADS * HEAD
+    d16 = dso[...]
+    cumc = cum[...]
+    ewt = jnp.exp(cumc[piece - 1 : piece] - cumc)
+    step = dt[...]
+    factor = ewt * step
+    facx = spread(factor)
+    xsf = xs[...].astype(F32)
+    t = mm(bm[...], d16)
+    dxs = skip[...] * dy[...].astype(F32) + facx * t + dxsd[...]
+    dfactor = gathered(xsf * t)
+    dbm = mm((xsf * facx).astype(B16), d16, NT) + dbmq[...]
+    dcm = dcm3[...] + dcmq[...]
+    dlog = dfactor * factor
+    states = jnp.sum(d16.astype(F32) * sin[...].astype(F32), 0, keepdims=True) * decay[0:1]
+    dend = gathered(jnp.broadcast_to(states, (8, inner)))[0:1]
+    dend = dend + jnp.sum(dlog, 0, keepdims=True)
+    dcum = dcum3[...] + dcumq[...] - dlog
+    last = lax.broadcasted_iota(jnp.int32, (piece, 128), 0) == piece - 1
+    dcum = dcum + jnp.where(last, dend, 0.0)
+    dda = mm(triangle(piece).astype(F32), dcum, TN, HIGHEST)
+    ddt = dfactor * ewt + ddtq[...] + dda * rate[...]
+    galog[...] = jnp.sum(dda * step, 0, keepdims=True) * rate[...]
+    dr = ddt * jax.nn.sigmoid(shift[...])
+    gdtb[...] = jnp.sum(dr, 0, keepdims=True)
+    draw[...] = dr.astype(B16)
+    padded = xbc[...].astype(F32)
+    for lo, hi, val in (
+        (0, inner, dxs),
+        (inner, inner + STATE, dbm),
+        (inner + STATE, inner + 2 * STATE, dcm),
+    ):
+        dp = val * silu_slope(pre[:, lo:hi])
+        dpre[:, lo:hi] = dp
+        gcb[:, lo:hi] = jnp.sum(dp, 0, keepdims=True)
+        for k in range(KCONV):
+            gconv[k : k + 1, lo:hi] = jnp.sum(
+                dp * padded[5 + k : 5 + k + piece, lo:hi], 0, keepdims=True
+            )
+
+
+def finish(dpre, after, conv, h, dz, draw, gin, tok, cot, norm, gw, gtok, gnorm):
+    piece = dpre.shape[0]
+    ext = jnp.concatenate([dpre[...], after[...]], 0)
+    dx = conv[KCONV - 1 : KCONV] * ext[:piece]
+    for k in range(KCONV - 1):
+        shift = KCONV - 1 - k
+        dx = dx + conv[k : k + 1] * ext[shift : shift + piece]
+    dx16 = dx.astype(B16)
+    inner = dz.shape[1]
+    spare = dpre.shape[1] - inner - 128
+    dzd = jnp.concatenate([dz[...], draw[...], jnp.zeros((piece, spare), B16)], 1)
+    gw[0] = mm(h[...], dx16, TN).astype(B16)
+    gw[1] = mm(h[...], dzd, TN).astype(B16)
+    dh = mm(dx16, gin[0], NT) + mm(dzd, gin[1], NT)
+    x = tok[...].astype(F32)
+    rinv = lax.rsqrt(jnp.mean(x * x, -1, keepdims=True) + EPS)
+    unit = x * rinv
+    gnorm[...] = jnp.sum(dh * unit, 0, keepdims=True)
+    du = dh * norm[...]
+    gtok[...] = (
+        cot[...].astype(F32) + rinv * (du - unit * jnp.mean(du * unit, -1, keepdims=True))
+    ).astype(B16)
 
 
 def body(
@@ -421,12 +677,13 @@
     chans = inner + 2 * STATE
     rows = in_weight.shape[0]
     orows = out_weight.shape[0]
-    edge_rows = KCONV - 1
+    edge_rows = 8
     spare = chans - inner - HEADS
     half = width // 2
     tokens = tokens[0]
     cotangent = cotangent[0]
 
+    before = passed_along(tokens[piece - edge_rows :], "seq", 1)
     win = jnp.stack(
         [
             in_weight[:, inner : inner + chans],
@@ -456,125 +713,83 @@
     conv_full = conv_full.reshape(KCONV, chans)
     cbias_full = gflat[:, cuts[2] : cuts[3]].reshape(-1)
     gnorm_full = gflat[:, cuts[3] : cuts[4]].reshape(-1)
-    w_x = gin[0].reshape(width, chans)
-    w_z = gin[1].reshape(width, chans)
-    w_o0 = gout[0].reshape(inner, half)
-    w_o1 = gout[1].reshape(inner, half)
-
-    x_in = tokens.astype(F32)
-    rinv = lax.rsqrt(jnp.mean(x_in * x_in, -1, keepdims=True) + EPS)
-    unit = x_in * rinv
-    h16 = (unit * norm_full).astype(B16)
-    xbc16 = dot("qd,de->qe", h16, w_x).astype(B16)
-    zd = dot("qd,de->qe", h16, w_z)
-    zval = zd[:, :inner]
-    dt_raw = zd[:, inner : inner + HEADS]
-    edge = passed_along(xbc16[piece - edge_rows :], "seq", 1)
-    padded16 = jnp.concatenate([edge, xbc16], 0)
-    pre = cbias_full + conv_full[0] * padded16[0:piece]
-    for k in range(1, KCONV):
-        pre = pre + conv_full[k] * padded16[k : k + piece]
-    xconv = jax.nn.silu(pre)
-    xs16 = xconv[:, :inner].astype(B16).reshape(piece, HEADS, HEAD)
-    bm16 = xconv[:, inner : inner + STATE].astype(B16)
-    cm16 = xconv[:, inner + STATE :].astype(B16)
-    shifted = dt_raw + dt_bias
-    dth = jax.nn.softplus(shifted).T
-    rate = -jnp.exp(a_log)
-    lower = jnp.arange(piece)[:, None] >= jnp.arange(piece)[None, :]
-    ones = lower.astype(F32)
-    highest = lax.Precision.HIGHEST
-    cumh = jnp.einsum("hu,tu->ht", dth * rate[:, None], ones, precision=highest)
-    seg = jnp.where(lower, cumh[:, :, None] - cumh[:, None, :], -1e30)
-    lmat = jnp.exp(seg)
-    gram = dot("tn,un->tu", cm16, bm16)
-    w16 = (gram[None] * lmat * dth[:, None, :]).astype(B16)
-    y_diag = dot("htu,uhp->thp", w16, xs16)
-    endc = cumh[:, -1]
-    ewt = jnp.exp(endc[:, None] - cumh)
-    factor = ewt * dth
-    bw16 = (bm16[None] * factor[..., None]).astype(B16)
-    s_loc = dot("hun,uhp->hpn", bw16, xs16)
-    decay = jnp.exp(endc)
-    s_in = carry_states(decay, s_loc, False)
-    s_in16 = s_in.astype(B16)
-    ecum = jnp.exp(cumh)
-    ce16 = (cm16[None] * ecum[..., None]).astype(B16)
-    y_off = dot("htn,hpn->thp", ce16, s_in16)
-    xsf = xs16.astype(F32)
-    yval = (y_diag + y_off + skip[:, None] * xsf).reshape(piece, inner)
-    gate_act = jax.nn.silu(zval)
-    gated = yval * gate_act
-    grinv = lax.rsqrt(jnp.mean(gated * gated, -1, keepdims=True) + EPS)
-    gunit = gated * grinv
-    n16 = (gunit * gnorm_full).astype(B16)
-    branch = jnp.concatenate([dot("qi,id->qd", n16, w_o0), dot("qi,id->qd", n16, w_o1)], -1)
-    mixed = (x_in + branch).astype(B16)
-    cot0 = cotangent[:, :half]
-    cot1 = cotangent[:, half:]
-    g_wout = jnp.stack(
-        [dot("qi,qd->id", n16, cot0).astype(B16), dot("qi,qd->id", n16, cot1).astype(B16)]
-    )
-    dnorm = dot("qd,id->qi", cot0, w_o0) + dot("qd,id->qi", cot1, w_o1)
-    g_gnorm = jnp.sum(dnorm * gunit, 0)
-    dscaled = dnorm * gnorm_full
-    dgated = grinv * (dscaled - gunit * jnp.mean(dscaled * gunit, -1, keepdims=True))
-    dy16 = (dgated * gate_act).astype(B16).reshape(piece, HEADS, HEAD)
-    dz = dgated * yval * silu_slope(zval)
-    dyf = dy16.astype(F32)
-    g_skip = jnp.sum(dyf * xsf, (0, 2))
-    dxs = skip[:, None] * dyf
-    dce = dot("thp,hpn->htn", dy16, s_in16)
-    ds_loc_in = dot("htn,thp->hpn", ce16, dy16)
-    dcm = jnp.sum(dce * ecum[..., None], 0)
-    dcum = jnp.sum(dce * cm16[None] * ecum[..., None], -1)
-    ds_out = carry_states(decay, ds_loc_in, True)
-    dsl16 = ds_out.astype(B16)
-    dend = jnp.sum(ds_out * s_in, (1, 2)) * decay
-    dbw = dot("hpn,uhp->hun", dsl16, xs16)
-    dxs = dxs + dot("hun,hpn->uhp", bw16, dsl16)
-    dbm = jnp.sum(dbw * factor[..., None], 0)
-    dfactor = jnp.sum(dbw * bm16[None], -1)
-    ddt = dfactor * ewt
-    dlog = dfactor * factor
-    dend = dend + jnp.sum(dlog, -1)
-    dcum = dcum - dlog
-    dwmat = dot("thp,uhp->htu", dy16, xs16)
-    dxs = dxs + dot("htu,thp->uhp", w16, dy16)
-    dlmat = dwmat * gram[None] * dth[:, None, :]
-    dg16 = jnp.sum(dwmat * lmat * dth[:, None, :], 0).astype(B16)
-    ddt = ddt + jnp.sum(dwmat * gram[None] * lmat, 1)
-    dseg = dlmat * lmat
-    dcum = dcum + jnp.sum(dseg, 2) - jnp.sum(dseg, 1)
-    dcm = dcm + dot("tu,un->tn", dg16, bm16)
-    dbm = dbm + dot("tu,tn->un", dg16, cm16)
-    dcum = dcum + jnp.pad(dend[:, None], ((0, 0), (piece - 1, 0)))
-    dda = jnp.einsum("ht,tu->hu", dcum, ones, precision=highest)
-    ddt = ddt + dda * rate[:, None]
-    g_alog = jnp.sum(dda * dth, 1) * rate
-    draw = ddt.T * jax.nn.sigmoid(shifted)
-    g_dtb = jnp.sum(draw, 0)
-    dxconv = jnp.concatenate([dxs.reshape(piece, inner), dbm, dcm], -1)
-    dpre = dxconv * silu_slope(pre)
-    g_cbias = jnp.sum(dpre, 0)
-    g_conv = jnp.stack([jnp.sum(dpre * padded16[k : k + piece], 0) for k in range(KCONV)])
-    dpadded = jnp.pad(conv_full[0] * dpre, ((0, edge_rows), (0, 0)))
-    for k in range(1, KCONV):
-        dpadded = dpadded + jnp.pad(conv_full[k] * dpre, ((k, edge_rows - k), (0, 0)))
-    returned = passed_along(dpadded[:edge_rows], "seq", -1)
-    dxbc = dpadded[edge_rows:] + jnp.pad(returned, ((piece - edge_rows, 0), (0, 0)))
-    dxbc16 = dxbc.astype(B16)
-    dzd16 = jnp.concatenate([dz, draw, jnp.zeros((piece, spare), F32)], -1).astype(B16)
-    g_win = jnp.stack(
-        [dot("qd,qe->de", h16, dxbc16).astype(B16), dot("qd,qe->de", h16, dzd16).astype(B16)]
-    )
-    dhid = dot("qe,de->qd", dxbc16, w_x) + dot("qe,de->qd", dzd16, w_z)
-    g_norm = jnp.sum(dhid * unit, 0)
-    dunit = dhid * norm_full
-    dx_in = cotangent.astype(F32) + rinv * (
-        dunit - unit * jnp.mean(dunit * unit, -1, keepdims=True)
-    )
-    grad_tokens = dx_in.astype(B16)
+    gin = gin.reshape(2, width, chans)
+    gout = gout.reshape(2, inner, half)
+    norm_full = norm_full[None]
+    cbias_full = cbias_full[None]
+    gnorm_full = gnorm_full[None]
+    lanes = ((0, 0), (0, 128 - HEADS))
+    dtb = jnp.pad(dt_bias[None], lanes)
+    rate = jnp.pad(-jnp.exp(a_log)[None], lanes)
+    skipx = jnp.repeat(skip, HEAD)[None]
+    tok_ext = jnp.concatenate([before, tokens], 0)
+    heads = ((piece, 128), F32)
+    wide = ((piece, inner), F32)
+    wide16 = ((piece, inner), B16)
+    thin16 = ((piece, STATE), B16)
+    thin = ((piece, STATE), F32)
+    state = ((STATE, inner), F32)
+    h16, xbc, pre, z, shift, dt, cum, xs, bm, cm, s_loc, decay = local_call(
+        project,
+        (
+            ((piece, width), B16),
+            ((piece + edge_rows, chans), B16),
+            ((piece, chans), F32),
+            wide,
+            heads,
+            heads,
+            heads,
+            wide16,
+            thin16,
+            thin16,
+            state,
+            ((8, inner), F32),
+        ),
+        *(tok_ext, norm_full, gin, conv_full, cbias_full, dtb, rate),
+    )
+    (ydiag,) = local_call(diagonal, (wide,), xs, bm, cm, dt, cum)
+    s_in = carry_states(decay[0:1], s_loc, False)
+    mixed, n16, dy, dz, g_gnorm, g_skip, dsl, dcm3, dcum3 = local_call(
+        gate,
+        (
+            ((piece, width), B16),
+            wide16,
+            wide16,
+            wide16,
+            ((1, inner), F32),
+            ((1, inner), F32),
+            state,
+            thin,
+            heads,
+        ),
+        *(tokens, s_in, ydiag, xs, cm, cum, z, skipx, gnorm_full, gout, cotangent),
+    )
+    dxsd, ddtq, dcumq, dcmq, dbmq, g_wout, _ = local_call(
+        diagonal_back,
+        (wide, heads, heads, thin, thin, ((2, inner, half), B16), ((128, piece), F32)),
+        *(xs, bm, cm, dt, cum, dy, n16, cotangent),
+    )
+    ds_out = carry_states(decay[0:1], dsl, True)
+    dpre, draw, g_dtb, g_alog, g_cbias, g_conv = local_call(
+        state_back,
+        (
+            ((piece, chans), F32),
+            ((piece, 128), B16),
+            ((1, 128), F32),
+            ((1, 128), F32),
+            ((1, chans), F32),
+            ((KCONV, chans), F32),
+        ),
+        *(ds_out, s_in, decay, xs, bm, dt, cum, dy, dxsd, ddtq, dcumq, dcmq, dbmq, dcum3, dcm3),
+        *(skipx, pre, xbc, shift, rate),
+    )
+    after = passed_along(dpre[:edge_rows], "seq", -1)
+    g_win, grad_tokens, g_norm = local_call(
+        finish,
+        (((2, width, chans), B16), ((piece, width), B16), ((1, width), F32)),
+        *(dpre, after, conv_full, h16, dz, draw, gin, tokens, cotangent, norm_full),
+    )
+    g_skip = jnp.sum(g_skip.reshape(HEADS, HEAD), 1)
 
     psmall = jnp.concatenate(
         [
@@ -586,7 +801,9 @@
         ],
         1,
     ).reshape(n, srows, 128)
-    phead = jnp.pad(jnp.stack([g_dtb, g_alog, g_skip]), ((0, 5), (0, 128 - HEADS)))
+    phead = jnp.pad(
+        jnp.concatenate([g_dtb, g_alog, jnp.pad(g_skip[None], lanes)], 0), ((0, 5), (0, 0))
+    )
     oin, oout, osmall, ohead = reduce_all(
         g_win.reshape(2, n, rows, chans), g_wout.reshape(2, n, orows, half), psmall, phead, n, ny
     )

time: 284 us -> 238 us (0.84)
  matrix products: 49.6 us -> 0 us
  Pallas kernels: 121 us -> 159 us
  other arithmetic: 33.9 us -> 3.59 us
  local copies, waits for them, and re-layouts: 37.1 us -> 24.7 us
  waiting for transfers between devices: 18.4 us -> 24.7 us
    dot_general x26 -> x0, matrix products: 49.6 us -> none  [the longest x24 49.1 us: dot(): return jnp.einsum(spec, left, right, preferred_element_type=F32)]
    pallas_call x0 -> x6, Pallas kernels: none -> 34 us  [local_call(): pl.pallas_call(kernel, out_shape=shapes, in_specs=[vmem] * len(args), out...]
    reduce_sum x8 -> x1, other arithmetic: 13.8 us -> 0.12 us  [body(): g_skip = jnp.sum(g_skip.reshape(HEADS, HEAD), 1)]
    unnamed x181 -> x92, local copies, waits for them, and re-layouts: 5.81 us -> 18 us
    another operation x5 -> x0, other arithmetic: 7.25 us -> none
    slice x8 -> x3, local copies, waits for them, and re-layouts: 7.94 us -> 0.79 us  [the longest x1 0.76 us: body(): before = passed_along(tokens[piece - edge_rows:], 'seq', 1)]
    ppermute x8, waiting for transfers between devices: 18.4 us -> 24.7 us  [passed_along(): return lax.ppermute(block, axis, route)]
    reshape x2 -> x3, local copies, waits for them, and re-layouts: 6.24 us -> 0.25 us  [the longest x1 0.09 us: body(): g_conv.reshape(KCONV, n, -1)]
  transfers between devices with their start and end apart: 8 -> 8, of which waited for: 3 -> 5; matrix products, arithmetic and copies ran while one was open for 8% -> 1% of each run, Pallas kernels for 0% -> 27%
where the time goes in v2:
time: 238 us; the launch traced here: 237 us
  Pallas kernels  159 us (67%)
  local copies, waits for them, and re-layouts  24.7 us (10%)
  waiting for transfers between devices  24.7 us (10%)
  starting transfers between devices  23.6 us (10%)
  other arithmetic  3.59 us (2%)
    pallas_call x1, Pallas kernels, reduce_all(): pl.pallas_call(functools.partial(reduce_kernel, n, ny), out_shape=(jax.Sh...  70.2 us
    pallas_call x1, Pallas kernels, gather_all(): pl.pallas_call(functools.partial(gather_kernel, n), out_shape=(jax.ShapeD...  55.1 us
    pallas_call x6, Pallas kernels, local_call(): pl.pallas_call(kernel, out_shape=shapes, in_specs=[vmem] * len(args), out...  34 us
    ppermute x8, waiting for transfers between devices, passed_along(): return lax.ppermute(block, axis, route)  24.7 us
    ppermute x8, starting transfers between devices, passed_along(): return lax.ppermute(block, axis, route)  23.6 us
    unnamed x92, local copies, waits for them, and re-layouts  18 us
  transfers between devices with their start and end apart: 8, of which 5 were waited for; matrix products, arithmetic and copies ran while one was open for 1% of the time, Pallas kernels for 27%

profile of v2, /device:TPU:0, one launch (start us, length us, event | category | flops | bytes accessed | tf_op | source)
XLA Modules:
  0.0 237.3 jit_solution(4989877018105964643)
XLA Ops:
  1.5 2.3 collective-permute-start
  5.7 55.1 %gather_weights.1 = (bf16[2,8,96,1792]{3,2,1,0:T(8,128)(2,1)S(1)}, bf16[2,8,192,384]{3,2,1,0:T(8,128)(2,1)S(1)}, f32[8,16,128]{2,1,0:T(8,128)S(1)}) custom-call(bf16[2,96,1792]{2,1,0:T(8,128)(2,1)S(1)} %pad_maximum_fusion.1.win, bf16[2,192,384]{2,1,0:T(8,128)(2,1)S(1)} %pad_maximum_fusion.4.wout, f32[16,128]{1,0:T(8,128)S(1)} %pad_bitcast_fusion.small), custom_call_target="tpu_custom_call" | custom-call | tf_op jit(solution)/shard_map/gather_weights/pallas_call | solution.py:122
  60.8 2.4 %copy-done.4 = bf16[2,8,96,1792]{3,2,1,0:T(8,128)(2,1)} copy-done((bf16[2,8,96,1792]{3,2,1,0:T(8,128)(2,1)}, bf16[2,8,96,1792]{3,2,1,0:T(8,128)(2,1)S(1)}, u32[]{:S(2)}) %copy-start.4) | copy-done | bytes 5505048
  63.2 1.4 copy-done.5
  65.3 6.6 %project.1 = (bf16[256,768]{1,0:T(8,128)(2,1)S(1)}, bf16[264,1792]{1,0:T(8,128)(2,1)S(1)}, f32[256,1792]{1,0:T(8,128)S(1)}, f32[256,1536]{1,0:T(8,128)S(1)}, f32...) custom-call(bf16[264,768]{1,0:T(8,128)(2,1)S(1)} %pad_maximum_fusion, ...), custom_call_target="tpu_custom_call" | custom-call | flops 5000000000 | bytes 5950464 | tf_op jit(solution)/shard_map/project/pallas_call | solution.py:447
  73.9 2.3 collective-permute-start.1
  76.2 1.3 collective-permute-done.1
  78.3 5.3 %collective-permute-start.2 = (bf16[128,1536]{1,0:T(8,128)(2,1)}, bf16[128,1536]{1,0:T(8,128)(2,1)S(1)}, u32[]{:S(2)}, u32[]{:S(2)}) collective-permute-start(bf16[128,1536]{1,0:T(8,128)(2,1)} %add_convert_fusion.4), channel_id=1, source_target_pairs={{0,1},{1,2},{2,3},{4,5},{5,6},{6,7},{8,9},{9,10},{10,11},{12,13},{... | collective-permute-start | bytes 1179656 | tf_op jit(solution)/shard_map/ppermute | solution.py:384
  85.3 8.1 %collective-permute-start.3 = (bf16[128,1536]{1,0:T(8,128)(2,1)S(1)}, bf16[128,1536]{1,0:T(8,128)(2,1)S(1)}, u32[]{:S(2)}, u32[]{:S(2)}) collective-permute-start(bf16[128,1536]{1,0:T(8,128)(2,1)S(1)} %add_convert_fusion.3), channel_id=1, source_target_pairs={{0,1},{1,2},{2,3},{4,5},{5,6},{6,7},{8,9},{9,10},{10,11},{12,13},{... | collective-permute-start | bytes 1179656 | tf_op jit(solution)/shard_map/ppermute | solution.py:384
  93.4 2.0 diagonal.1.ydiag
  95.5 7.4 %gate.1 = (bf16[256,768]{1,0:T(8,128)(2,1)}, bf16[256,1536]{1,0:T(8,128)(2,1)S(1)}, bf16[256,1536]{1,0:T(8,128)(2,1)S(1)}, bf16[256,1536]{1,0:T(8,128)(2,1)S(1)}...) custom-call(bf16[256,768]{1,0:T(8,128)(2,1)S(1)} %bitcast.55, ...), custom_call_target="tpu_custom_call" | custom-call | flops 5000000000 | bytes 7680000 | tf_op jit(solution)/shard_map/gate/pallas_call | solution.py:447
  103.0 1.3 collective-permute-start.4
  104.3 6.6 %collective-permute-done.4 = bf16[128,1536]{1,0:T(8,128)(2,1)S(1)} collective-permute-done((bf16[128,1536]{1,0:T(8,128)(2,1)S(1)}, bf16[128,1536]{1,0:T(8,128)(2,1)S(1)}, u32[]{:S(2)}, u32[]{:S(2)}) %collective-permute-start.4) | collective-permute-done | bytes 393248 | tf_op jit(solution)/shard_map/ppermute | solution.py:384
  111.0 1.3 collective-permute-start.5
  112.6 8.2 %collective-permute-done.5 = bf16[128,1536]{1,0:T(8,128)(2,1)S(1)} collective-permute-done((bf16[128,1536]{1,0:T(8,128)(2,1)S(1)}, bf16[128,1536]{1,0:T(8,128)(2,1)S(1)}, u32[]{:S(2)}, u32[]{:S(2)}) %collective-permute-start.5) | collective-permute-done | bytes 393248 | tf_op jit(solution)/shard_map/ppermute | solution.py:384
  121.0 1.5 collective-permute-start.6
  126.2 7.2 %diagonal_back.1 = (f32[256,1536]{1,0:T(8,128)S(1)}, f32[256,128]{1,0:T(8,128)S(1)}, f32[256,128]{1,0:T(8,128)S(1)}, f32[256,128]{1,0:T(8,128)S(1)}, f32[256,128...) custom-call(bf16[256,1536]{1,0:T(8,128)(2,1)S(1)} %copy-done.18, ...), custom_call_target="tpu_custom_call" | custom-call | flops 5000000000 | bytes 3145728 | tf_op jit(solution)/shard_map/diagonal_back/pallas_call | solution.py:447
  133.5 3.9 %state_back.1 = (f32[256,1792]{1,0:T(8,128)S(1)}, bf16[256,128]{1,0:T(8,128)(2,1)S(1)}, f32[1,128]{1,0:T(1,128)S(1)}, f32[1,128]{1,0:T(1,128)S(1)}, f32[1,1792]{1,0:T(1,128)S(1)}, /*index=5*/f32[4,1792]{1,0:T(4,128)S(1)}) custom-call(bf16[128,1536]{1,0:T(8,128)(2,1)S(1)} %collective-permute-done.6.dso, bf16[128,1536]{1,0:T(8,128)(2,1)S(1)} %copy-done.8, ...), custom_call_target="tpu_custom_call" | custom-call | flops 5000000000 | bytes 8014336 | tf_op jit(solution)/shard_map/state_back/pallas_call | solution.py:447
  138.7 1.5 collective-permute-start.7
  140.6 7.3 %collective-permute-done.7.after = f32[8,1792]{1,0:T(8,128)S(1)} collective-permute-done((f32[8,1792]{1,0:T(8,128)S(1)}, f32[8,1792]{1,0:T(8,128)S(1)}, u32[]{:S(2)}, u32[]{:S(2)}) %collective-permute-start.7) | collective-permute-done | bytes 57376 | tf_op jit(solution)/shard_map/ppermute | solution.py:384
  147.9 1.5 copy-done.3
  152.4 6.9 %finish.1 = (bf16[2,768,1792]{2,1,0:T(8,128)(2,1)S(1)}, bf16[256,768]{1,0:T(8,128)(2,1)}, f32[1,768]{1,0:T(1,128)S(1)}) custom-call(f32[256,1792]{1,0:T(8,128)S(1)} %copy-done.3, f32[8,1792]{1,0:T(8,128)S(1)} %collective-permute-done.7.after, f32[4,1792]{1,0:T(4,128)S(1)} %reshape.83.conv, bf16[256,768]{1,0:T(8,128)(2,1)S(1)} %copy-done.24, ...), custom_call_target="tpu_custom_call" | custom-call | flops 5000000000 | bytes 9460736 | tf_op jit(solution)/shard_map/finish/pallas_call | solution.py:447
  159.3 2.4 %copy-done = bf16[2,768,1792]{2,1,0:T(8,128)(2,1)} copy-done((bf16[2,768,1792]{2,1,0:T(8,128)(2,1)}, bf16[2,768,1792]{2,1,0:T(8,128)(2,1)S(1)}, u32[]{:S(2)}) %copy-start) | copy-done | bytes 5505048
  161.9 70.2 %reduce_gradients.1 = (f32[2,96,1792]{2,1,0:T(8,128)S(1)}, f32[2,192,384]{2,1,0:T(8,128)S(1)}, f32[16,128]{1,0:T(8,128)S(1)}, f32[8,128]{1,0:T(8,128)S(1)}) custom-call(bf16[2,8,96,1792]{3,2,1,0:T(8,128)(2,1)} %bitcast.52, bf16[2,8,192,384]{3,2,1,0:T(8,128)(2,1)S(1)} %bitcast.53, f32[8,16,128]{2,1,0:T(8,128)S(1)} %bitcast.57, f32[8,128]{1,0:T(8,128)S(1)} %pad.22.phead), custom_call_target="tpu_custom_call" | custom-call | tf_op jit(solution)/shard_map/reduce_gradients/pallas_call | solution.py:335
  (159 shorter events, 21.7 us)
Async XLA Ops:
  1.5 63.8 %collective-permute-start = (bf16[8,768]{1,0:T(8,128)(2,1)S(1)}, bf16[8,768]{1,0:T(8,128)(2,1)S(1)}, u32[]{:S(2)}, u32[]{:S(2)}) collective-permute-start(bf16[8,768]{1,0:T(8,128)(2,1)S(1)} %slice_bitcast_fusion.8), channel_id=1, source_target_pairs={{0,1},{1,2},{2,3},{4,5},{5,6},{6,7},{8,9},{9,10},{10,11},{12,13},{... | collective-permute-start | bytes 36872 | tf_op jit(solution)/shard_map/ppermute | solution.py:384
  5.2 60.0 %copy-start.44 = (f32[24]{0:T(128)S(1)}, f32[24]{0:T(128)}, u32[]{:S(2)}) copy-start(f32[24]{0:T(128)} %param.16) | copy-start | bytes 292
  5.2 60.0 %copy-start.1 = (bf16[1,256,768]{2,1,0:T(8,128)(2,1)S(1)}, bf16[1,256,768]{2,1,0:T(8,128)(2,1)}, u32[]{:S(2)}) copy-start(bf16[1,256,768]{2,1,0:T(8,128)(2,1)} %param.11) | copy-start | bytes 1179652
  73.8 19.6 %copy-start.33 = (bf16[256,128]{1,0:T(8,128)(2,1)}, bf16[256,128]{1,0:T(8,128)(2,1)S(1)}, u32[]{:S(2)}) copy-start(bf16[256,128]{1,0:T(8,128)(2,1)S(1)} %get-tuple-element.59.bm) | copy-start | bytes 196612
  73.8 21.7 %copy-start.17 = (bf16[256,1536]{1,0:T(8,128)(2,1)}, bf16[256,1536]{1,0:T(8,128)(2,1)S(1)}, u32[]{:S(2)}) copy-start(bf16[256,1536]{1,0:T(8,128)(2,1)S(1)} %get-tuple-element.58.xs) | copy-start | bytes 2359300
  73.8 21.7 %copy-start.25 = (f32[256,128]{1,0:T(8,128)}, f32[256,128]{1,0:T(8,128)S(1)}, u32[]{:S(2)}) copy-start(f32[256,128]{1,0:T(8,128)S(1)} %get-tuple-element.62.cum) | copy-start | bytes 393220
  73.8 21.7 %copy-start.35 = (bf16[256,128]{1,0:T(8,128)(2,1)}, bf16[256,128]{1,0:T(8,128)(2,1)S(1)}, u32[]{:S(2)}) copy-start(bf16[256,128]{1,0:T(8,128)(2,1)S(1)} %get-tuple-element.60.cm) | copy-start | bytes 196612
  73.8 10.0 %copy-start.41 = (f32[24]{0:T(128)S(1)}, f32[24]{0:T(128)}, u32[]{:S(2)}) copy-start(f32[24]{0:T(128)} %param.18) | copy-start | bytes 292
  73.9 3.6 %collective-permute-start.1 = (bf16[128,1536]{1,0:T(8,128)(2,1)S(1)}, bf16[128,1536]{1,0:T(8,128)(2,1)S(1)}, u32[]{:S(2)}, u32[]{:S(2)}) collective-permute-start(bf16[128,1536]{1,0:T(8,128)(2,1)S(1)} %add_convert_fusion.5), channel_id=1, source_target_pairs={{0,1},{1,2},{2,3},{4,5},{5,6},{6,7},{8,9},{9,10},{10,11},{12,13},{... | collective-permute-start | bytes 1179656 | tf_op jit(solution)/shard_map/ppermute | solution.py:384
  78.3 6.8 %collective-permute-start.2 = (bf16[128,1536]{1,0:T(8,128)(2,1)}, bf16[128,1536]{1,0:T(8,128)(2,1)S(1)}, u32[]{:S(2)}, u32[]{:S(2)}) collective-permute-start(bf16[128,1536]{1,0:T(8,128)(2,1)} %add_convert_fusion.4), channel_id=1, source_target_pairs={{0,1},{1,2},{2,3},{4,5},{5,6},{6,7},{8,9},{9,10},{10,11},{12,13},{... | collective-permute-start | bytes 1179656 | tf_op jit(solution)/shard_map/ppermute | solution.py:384
  85.3 10.1 %collective-permute-start.3 = (bf16[128,1536]{1,0:T(8,128)(2,1)S(1)}, bf16[128,1536]{1,0:T(8,128)(2,1)S(1)}, u32[]{:S(2)}, u32[]{:S(2)}) collective-permute-start(bf16[128,1536]{1,0:T(8,128)(2,1)S(1)} %add_convert_fusion.3), channel_id=1, source_target_pairs={{0,1},{1,2},{2,3},{4,5},{5,6},{6,7},{8,9},{9,10},{10,11},{12,13},{... | collective-permute-start | bytes 1179656 | tf_op jit(solution)/shard_map/ppermute | solution.py:384
  95.4 7.4 %copy-start.7 = (bf16[128,1536]{1,0:T(8,128)(2,1)}, bf16[128,1536]{1,0:T(8,128)(2,1)S(1)}, u32[]{:S(2)}) copy-start(bf16[128,1536]{1,0:T(8,128)(2,1)S(1)} %collective-permute-done.3.sin) | copy-start | bytes 1179652
  102.9 8.1 %copy-start.13 = (bf16[256,1536]{1,0:T(8,128)(2,1)}, bf16[256,1536]{1,0:T(8,128)(2,1)S(1)}, u32[]{:S(2)}) copy-start(bf16[256,1536]{1,0:T(8,128)(2,1)S(1)} %get-tuple-element.81.dz) | copy-start | bytes 2359300
  102.9 8.1 %copy-start.19 = (bf16[256,1536]{1,0:T(8,128)(2,1)}, bf16[256,1536]{1,0:T(8,128)(2,1)S(1)}, u32[]{:S(2)}) copy-start(bf16[256,1536]{1,0:T(8,128)(2,1)S(1)} %get-tuple-element.67.dy) | copy-start | bytes 2359300
  102.9 8.1 %copy-start.21 = (bf16[256,1536]{1,0:T(8,128)(2,1)}, bf16[256,1536]{1,0:T(8,128)(2,1)S(1)}, u32[]{:S(2)}) copy-start(bf16[256,1536]{1,0:T(8,128)(2,1)S(1)} %get-tuple-element.68.normed) | copy-start | bytes 2359300
  102.9 8.1 %copy-start.27 = (f32[256,128]{1,0:T(8,128)}, f32[256,128]{1,0:T(8,128)S(1)}, u32[]{:S(2)}) copy-start(f32[256,128]{1,0:T(8,128)S(1)} %get-tuple-element.75.dcm3) | copy-start | bytes 393220
  102.9 8.1 %copy-start.29 = (f32[256,128]{1,0:T(8,128)}, f32[256,128]{1,0:T(8,128)S(1)}, u32[]{:S(2)}) copy-start(f32[256,128]{1,0:T(8,128)S(1)} %get-tuple-element.74.dcum3) | copy-start | bytes 393220
  103.0 7.9 %collective-permute-start.4 = (bf16[128,1536]{1,0:T(8,128)(2,1)S(1)}, bf16[128,1536]{1,0:T(8,128)(2,1)S(1)}, u32[]{:S(2)}, u32[]{:S(2)}) collective-permute-start(bf16[128,1536]{1,0:T(8,128)(2,1)S(1)} %add_convert_fusion.2), channel_id=1, source_target_pairs={{1,0},{2,1},{3,2},{5,4},{6,5},{7,6},{9,8},{10,9},{11,10},{13,12},{... | collective-permute-start | bytes 1179656 | tf_op jit(solution)/shard_map/ppermute | solution.py:384
  111.0 9.8 %collective-permute-start.5 = (bf16[128,1536]{1,0:T(8,128)(2,1)S(1)}, bf16[128,1536]{1,0:T(8,128)(2,1)S(1)}, u32[]{:S(2)}, u32[]{:S(2)}) collective-permute-start(bf16[128,1536]{1,0:T(8,128)(2,1)S(1)} %add_convert_fusion.1), channel_id=1, source_target_pairs={{1,0},{2,1},{3,2},{5,4},{6,5},{7,6},{9,8},{10,9},{11,10},{13,12},{... | collective-permute-start | bytes 1179656 | tf_op jit(solution)/shard_map/ppermute | solution.py:384
  112.6 9.8 %copy-start.20 = (bf16[256,1536]{1,0:T(8,128)(2,1)S(1)}, bf16[256,1536]{1,0:T(8,128)(2,1)}, u32[]{:S(2)}) copy-start(bf16[256,1536]{1,0:T(8,128)(2,1)} %copy-done.19) | copy-start | bytes 2359300
  112.6 9.9 %copy-start.22 = (bf16[256,1536]{1,0:T(8,128)(2,1)S(1)}, bf16[256,1536]{1,0:T(8,128)(2,1)}, u32[]{:S(2)}) copy-start(bf16[256,1536]{1,0:T(8,128)(2,1)} %copy-done.21) | copy-start | bytes 2359300
  121.0 12.5 %collective-permute-start.6 = (bf16[128,1536]{1,0:T(8,128)(2,1)S(1)}, bf16[128,1536]{1,0:T(8,128)(2,1)S(1)}, u32[]{:S(2)}, u32[]{:S(2)}) collective-permute-start(bf16[128,1536]{1,0:T(8,128)(2,1)S(1)} %add_convert_fusion), channel_id=1, source_target_pairs={{1,0},{2,1},{3,2},{5,4},{6,5},{7,6},{9,8},{10,9},{11,10},{13,12},{... | collective-permute-start | bytes 1179656 | tf_op jit(solution)/shard_map/ppermute | solution.py:384
  126.2 7.2 %copy-start.30 = (f32[256,128]{1,0:T(8,128)S(1)}, f32[256,128]{1,0:T(8,128)}, u32[]{:S(2)}) copy-start(f32[256,128]{1,0:T(8,128)} %copy-done.29) | copy-start | bytes 393220
  138.7 9.2 %collective-permute-start.7 = (f32[8,1792]{1,0:T(8,128)S(1)}, f32[8,1792]{1,0:T(8,128)S(1)}, u32[]{:S(2)}, u32[]{:S(2)}) collective-permute-start(f32[8,1792]{1,0:T(8,128)S(1)} %slice.88), channel_id=1, source_target_pairs={{1,0},{2,1},{3,2},{5,4},{6,5},{7,6},{9,8},{10,9},{11,10},{13,12},{... | collective-permute-start | bytes 172040 | tf_op jit(solution)/shard_map/ppermute | solution.py:384
  (31 other events, 86.3 us)
